TPU v7x, 32 devices: a whole 2x2x4 slice. The times are simulated.
32 devices in a mesh: dp: 4 (over x, core), expert: 8 (over z, y).
Axes of the slice: x: 2, y: 2, z: 4, core: 2. Of those that a mesh axis runs over, the one named last changes fastest.
Arguments:
- tokens: bfloat16 [8192, 1024], P(('dp', 'expert')), may hold values from -6 to 6
- gain_attn: bfloat16 [1024], P(('dp', 'expert')), may hold values from 0.5 to 1.5
- w_query: bfloat16 [1024, 1024], P(('dp', 'expert')), may hold values from -0.1875 to 0.1875
- w_key: bfloat16 [1024, 1024], P(('dp', 'expert')), may hold values from -0.1875 to 0.1875
- w_value: bfloat16 [1024, 1024], P(('dp', 'expert')), may hold values from -0.1875 to 0.1875
- w_output: bfloat16 [1024, 1024], P(('dp', 'expert')), may hold values from -1.5 to 1.5
- rel_bias: float32 [32, 16], replicated, may hold values from -4 to 4
- gain_ffn: bfloat16 [1024], P(('dp', 'expert')), may hold values from 0.5 to 1.5
- w_router: bfloat16 [1024, 8], P(('dp', 'expert')), may hold values from -0.125 to 0.125
- expert_gate: bfloat16 [8, 1024, 2816], P('expert', 'dp'), may hold values from -0.1875 to 0.1875
- expert_up: bfloat16 [8, 1024, 2816], P('expert', 'dp'), may hold values from -0.1875 to 0.1875
- expert_down: bfloat16 [8, 2816, 1024], P('expert', 'dp'), may hold values from -0.21875 to 0.21875
- routes: int32 [8192, 2], P(('dp', 'expert')), may hold values from 0 to 7, all different within a row; in each aligned block of 256 rows (0 to 255, 256 to 511, ...) at most 80 rows name the same one
- doc_lengths: int32 [4, 4], replicated, may hold values from 1 to 1792, 2048 in all within a row
- seq_valid: int32 [4], replicated, may hold values from 1536 to 2048
- grad_output: bfloat16 [8192, 1024], P(('dp', 'expert')), may hold values from -6 to 6
Outputs:
- mixed: bfloat16 [8192, 1024], P(('dp', 'expert'))
- grad_tokens: float32 [8192, 1024], P(('dp', 'expert'))
- grad_gain_attn: float32 [1024], P(('dp', 'expert'))
- grad_query: float32 [1024, 1024], P(('dp', 'expert'))
- grad_key: float32 [1024, 1024], P(('dp', 'expert'))
- grad_value: float32 [1024, 1024], P(('dp', 'expert'))
- grad_w_output: float32 [1024, 1024], P(('dp', 'expert'))
- grad_rel_bias: float32 [32, 16], replicated
- grad_gain_ffn: float32 [1024], P(('dp', 'expert'))
- grad_router: float32 [1024, 8], P(('dp', 'expert'))
- grad_expert_gate: float32 [8, 1024, 2816], P('expert', 'dp')
- grad_expert_up: float32 [8, 1024, 2816], P('expert', 'dp')
- grad_expert_down: float32 [8, 2816, 1024], P('expert', 'dp')
- head_factor: float32 [16], replicated
Inputs may be any that keep to these rules, and one draw needn't show every extreme that they name: `routes`: each row names 2 different experts; among the tokens of one device no expert is named more than 80 times, and some device names some expert exactly 80 times. `doc_lengths`: each row sums to 2048.
All inputs are finite; a program needn't handle non-finite values.
Results may differ from a plain program's by a relative error of at most 0.015.
Values may be sent and summed in bfloat16 or wider, within the bound.
No kernel may reach another device: no remote copies, remote signals or barrier semaphores. Data moves between devices by JAX's collectives and lax.ppermute only.
A program may use at most 448 MiB of HBM per device.

v0:
```python
import jax
import jax.numpy as jnp
import numpy as np
from jax import lax
from jax.experimental import pallas as pl
from jax.experimental.pallas import tpu as pltpu
from jax.sharding import PartitionSpec as P

HEADS = 16
HDIM = 64
BUCKETS = 32
WINDOW = 1024
SEQ = 2048
DOCS = 4
TOP = 2

EPSILON = 1e-06
CLIP_LEVEL = 4.0
BF = jnp.bfloat16
F32 = jnp.float32
MASKED = -1e30
AUX = 128
ROUTER_AT = 2
GAIN_AT = 63
BIAS_AT = 64
TOP_AT = 96
TOP_LOW_AT = 112


def dot(left, right, dims=((1,), (0,))):
    return lax.dot_general(left, right, (dims, ((), ())), preferred_element_type=F32)


def halves(values):
    high = values.astype(BF)
    return high, (values - high.astype(F32)).astype(BF)


def call(kernel, out_shape, flops, nbytes, mib=56, **kwargs):
    return pl.pallas_call(
        kernel,
        out_shape=out_shape,
        compiler_params=pltpu.CompilerParams(vmem_limit_bytes=mib * 1024 * 1024),
        cost_estimate=pl.CostEstimate(
            flops=int(flops), bytes_accessed=int(nbytes), transcendentals=0
        ),
        **kwargs,
    )


def struct(shape, dtype):
    return jax.ShapeDtypeStruct(shape, dtype)


def bucket_of(span, buckets):
    distance = np.arange(span) * 1.0
    exact = buckets // 2
    safe = np.maximum(distance, 1.0)
    spread = exact + np.floor(np.log(safe / exact) / np.log(128.0 / exact) * (buckets - exact))
    return np.where(distance < exact, distance, np.minimum(spread, buckets - 1.0)).astype(np.int64)


def diagonal_tables(block, window, buckets):
    tiles = window // block + 1
    j = np.arange(2 * block)
    offset = np.where(j < block, -j, 2 * block - j)
    distance = np.arange(tiles)[:, None] * block + offset[None, :]
    inside = (distance >= 0) & (distance < window) & (j != block)[None, :]
    bucket = bucket_of(window, buckets)[np.clip(distance, 0, window - 1)]
    marks = (bucket[..., None] == np.arange(buckets)) & inside[..., None]
    return marks.astype(np.float32).reshape(-1, buckets), inside.reshape(-1)


def collect(parts, me, whole, arrived):
    for j, part in enumerate(parts):
        pltpu.make_async_copy(part, whole.at[me ^ j], arrived.at[j]).start()


def collected(parts, whole, arrived):
    for j, part in enumerate(parts):
        pltpu.make_async_copy(part, whole.at[0], arrived.at[j]).wait()


def part_copies(parts, source, first, rows, to, semaphore):
    cut = parts[-1].shape[0]
    if cut == parts[0].shape[0] or source < len(parts) - 2:
        return [pltpu.make_async_copy(parts[source].at[pl.ds(first, rows)], to, semaphore)]
    copies = []
    low = max(0, min(rows, cut - first))
    if low:
        copies.append(
            pltpu.make_async_copy(
                parts[source].at[pl.ds(first, low)], to.at[pl.ds(0, low)], semaphore
            )
        )
    if low < rows:
        copies.append(
            pltpu.make_async_copy(
                parts[source + 1].at[pl.ds(first + low - cut, rows - low)],
                to.at[pl.ds(low, rows - low)],
                semaphore,
            )
        )
    return copies


def gain_row(aux, at):
    rows = lax.broadcasted_iota(jnp.int32, (8, AUX), 0)
    lanes = lax.broadcasted_iota(jnp.int32, (8, AUX), 1)
    pick = jnp.where((rows == 0) & (lanes == at), 1.0, 0.0).astype(BF)
    return dot(pick, aux, ((1,), (1,)))[0:1]


def head_lanes(rows, lanes, head):
    lane = lax.broadcasted_iota(jnp.int32, (rows, lanes), 1)
    return lane // HDIM == head


def fold(values, combine):
    parts = [values[:, at : at + 128] for at in range(0, values.shape[1], 128)]
    total = parts[0]
    for part in parts[1:]:
        total = combine(total, part)
    return total


def attend_kernel(tiles, hp, sources, spread, pick_ref, me_ref, *refs):
    tok_refs = refs[:sources]
    w_refs = refs[sources : sources + spread]
    (diag_ref, ends_ref, normed_ref, qkv_ref, p_ref, out_ref, top_ref, aux_ref,
     bias, keys, values, tok, arrived, packed, w_arrived, gain) = refs[sources + spread :]
    i = pl.program_id(0)
    block, lanes = out_ref.shape
    width = normed_ref.shape[1]

    @pl.when(i == 0)
    def _():
        collect(w_refs, me_ref[0], packed, w_arrived)
        for at in range(tok.shape[0]):
            for source in range(sources - (tok_refs[-1].shape[0] != tok_refs[0].shape[0])):
                @pl.when(pick_ref[at] == source)
                def _():
                    for copy in part_copies(
                        tok_refs, source, 0, block, tok.at[at], arrived.at[at]
                    ):
                        copy.start()
        for h in range(hp):
            for m in range(tiles):
                at = h * tiles + m
                row = jnp.broadcast_to(diag_ref[at : at + 1, :], (block, 2 * block))
                at = (tiles - 1 - m) * block
                bias[h, :, at : at + block] = pltpu.roll(
                    row, 0, 1, stride=1, stride_axis=0
                )[:, :block]
        top_ref[...] = jnp.full_like(top_ref, MASKED)
        collected(w_refs, packed, w_arrived)
        aux_ref[...] = packed[:, :, 3 * lanes :].reshape(width, AUX)
        gain[...] = gain_row(aux_ref[...], 0)

    pltpu.make_async_copy(tok_refs[0].at[pl.ds(0, block)], tok.at[i], arrived.at[i]).wait()
    x = tok[i].astype(F32)
    r = lax.rsqrt(jnp.mean(x * x, axis=1, keepdims=True) + EPSILON)
    normed = (x * r * gain[...]).astype(BF)
    normed_ref[...] = normed
    w_cols = packed[:, :, : 3 * lanes].reshape(width, 3 * lanes)
    qkv = dot(normed, w_cols).astype(BF)
    qkv_ref[...] = qkv
    here = pl.multiple_of(i * block, block)
    keys[pl.ds(here, block), :] = qkv[:, lanes : 2 * lanes]
    values[pl.ds(here, block), :] = qkv[:, 2 * lanes :]
    query = qkv[:, :lanes] * jnp.asarray(HDIM ** -0.5, BF)
    masks = [head_lanes(block, lanes, h) for h in range(hp)]
    heads = [jnp.where(masks[h], query, jnp.zeros_like(query)) for h in range(hp)]

    def label_of(positions):
        label = jnp.zeros(positions.shape, jnp.int32)
        for at in range(DOCS):
            label += jnp.where(positions >= ends_ref[at], 1, 0)
        return label

    qlab = label_of(lax.broadcasted_iota(jnp.int32, (block, 1), 0) + i * block)

    def rows_of(span):
        wide = span * block
        first = pl.multiple_of((i - span + 1) * block, block)
        column = (tiles - span) * block
        key = keys[pl.ds(first, wide), :]
        value = values[pl.ds(first, wide), :]
        position = lax.broadcasted_iota(jnp.int32, (1, wide), 1) + first
        same = qlab == jnp.where(position < ends_ref[DOCS], label_of(position), -1)
        row = lax.broadcasted_iota(jnp.int32, (block, block), 0)
        diagonal = row == lax.broadcasted_iota(jnp.int32, (block, block), 1)
        out = None
        for h in range(hp):
            s = dot(heads[h], key, ((1,), (1,))) + bias[h, :, column:]
            last = wide - block
            own = jnp.where(same[:, last:] | diagonal, s[:, last:], MASKED)
            if span > 1:
                own = jnp.concatenate([jnp.where(same[:, :last], s[:, :last], MASKED), own], axis=1)
            best = jnp.max(own, axis=1, keepdims=True)
            top_ref[h : h + 1, :] = jnp.maximum(
                top_ref[h : h + 1, :], jnp.max(best, axis=0, keepdims=True)
            )
            p = jnp.exp(own - best)
            p = (p * (1.0 / jnp.sum(p, axis=1, keepdims=True))).astype(BF)
            p_ref[0, h, :, column:] = p
            part = dot(p, value)
            out = part if out is None else jnp.where(masks[h], part, out)
        out_ref[...] = out.astype(BF)

    for span in range(1, tiles):
        @pl.when(i == span - 1)
        def _():
            rows_of(span)

    @pl.when(i >= tiles - 1)
    def _():
        rows_of(tiles)


def attend(pick, me, parts, packed, diag, ends, hp, block):
    width = parts[0].shape[1]
    count = pick.shape[0]
    seq = count * block
    lanes = hp * HDIM
    tiles = diag.shape[0] // hp
    row = lambda i: (i, 0)
    fixed = lambda i: (0, 0)
    pairs = count * tiles * hp * block * block
    return call(
        lambda *refs: attend_kernel(tiles, hp, len(parts), len(packed), *refs),
        (
            struct((seq, width), BF),
            struct((seq, 3 * lanes), BF),
            struct((count, hp, block, tiles * block), BF),
            struct((seq, lanes), BF),
            struct((8, 128), F32),
            struct((width, AUX), BF),
        ),
        24e9,
        8 * seq * width + 2 * pairs,
        grid=(count,),
        in_specs=[pl.BlockSpec(memory_space=pltpu.SMEM)] * 2
        + [pl.BlockSpec(memory_space=pl.ANY)] * (len(parts) + len(packed))
        + [
            pl.BlockSpec(diag.shape, fixed),
            pl.BlockSpec(memory_space=pltpu.SMEM),
        ],
        out_specs=[
            pl.BlockSpec((block, width), row),
            pl.BlockSpec((block, 3 * lanes), row),
            pl.BlockSpec((1, hp, block, tiles * block), lambda i: (i, 0, 0, 0)),
            pl.BlockSpec((block, lanes), row),
            pl.BlockSpec((8, 128), fixed),
            pl.BlockSpec((width, AUX), fixed),
        ],
        scratch_shapes=[
            pltpu.VMEM((hp, block, tiles * block), F32),
            pltpu.VMEM((seq, lanes), BF),
            pltpu.VMEM((seq, lanes), BF),
            pltpu.VMEM((count, block, width), BF),
            pltpu.SemaphoreType.DMA((count,)),
            pltpu.VMEM((len(packed),) + packed[0].shape, BF),
            pltpu.SemaphoreType.DMA((len(packed),)),
            pltpu.VMEM((1, width), F32),
        ],
    )(pick, me, *parts, *packed, diag, ends)


def output_rows_kernel(sources, first, rows, pick_ref, *refs):
    parts = refs[:sources]
    out_ref, qkv_ref, arrived = refs[sources:]
    width = out_ref.shape[1]

    def place(at, number):
        here = pl.ds(at * rows, rows)
        if number == 0:
            return out_ref.at[here]
        return qkv_ref.at[here, pl.ds((number - 1) * width, width)]

    for at in range(pick_ref.shape[0]):
        for source in range(len(parts) - (parts[-1].shape[0] != parts[0].shape[0])):
            @pl.when(pick_ref[at] == source)
            def _():
                for number in range(4):
                    for copy in part_copies(
                        parts, source, first + number * rows, rows, place(at, number),
                        arrived.at[at, number],
                    ):
                        copy.start()
    for at in range(pick_ref.shape[0]):
        for number in range(4):
            pltpu.make_async_copy(
                parts[0].at[pl.ds(0, rows)], place(at, number), arrived.at[at, number]
            ).wait()


def attend_back_kernel(tiles, hp, me_ref, grad_ref, p_ref, qkv_ref, normed_ref, marks_ref, top_ref,
                       out_ref, kept_ref, away_ref, bias_grad, key_grad, value_grad):
    i = pl.program_id(0)
    block, lanes = grad_ref.shape

    @pl.when(i == 0)
    def _():
        bias_grad[...] = jnp.zeros_like(bias_grad)
        key_grad[...] = jnp.zeros_like(key_grad)
        value_grad[...] = jnp.zeros_like(value_grad)

    here = pl.multiple_of(i * block, block)
    query = qkv_ref[pl.ds(here, block), :lanes] * jnp.asarray(HDIM ** -0.5, BF)
    grad = grad_ref[...]
    masks = [head_lanes(block, lanes, h) for h in range(hp)]

    def rows_of(span):
        wide = span * block
        first = pl.multiple_of((i - span + 1) * block, block)
        column = (tiles - span) * block
        key = qkv_ref[pl.ds(first, wide), lanes : 2 * lanes]
        value = qkv_ref[pl.ds(first, wide), 2 * lanes :]
        out = key_part = value_part = None
        for h in range(hp):
            head = jnp.where(masks[h], query, jnp.zeros_like(query))
            head_grad = jnp.where(masks[h], grad, jnp.zeros_like(grad))
            weight = p_ref[0, h, :, column:]
            wide_weight = weight.astype(F32)
            t = wide_weight * dot(head_grad, value, ((1,), (1,)))
            s = t - wide_weight * jnp.sum(t, axis=1, keepdims=True)
            bias_grad[h, :, column:] += s
            s = s.astype(BF)
            part = dot(s, key)
            out = part if out is None else jnp.where(masks[h], part, out)
            part = dot(s, head, ((0,), (0,)))
            key_part = part if key_part is None else key_part + part
            part = dot(weight, head_grad, ((0,), (0,)))
            value_part = part if value_part is None else value_part + part
        key_grad[pl.ds(first, wide), :] += key_part
        value_grad[pl.ds(first, wide), :] += value_part
        out_ref[pl.ds(here, block), :lanes] = (out * HDIM ** -0.5).astype(BF)

    for span in range(1, tiles):
        @pl.when(i == span - 1)
        def _():
            rows_of(span)

    @pl.when(i >= tiles - 1)
    def _():
        rows_of(tiles)

    @pl.when(i == pl.num_programs(0) - 1)
    def _():
        out_ref[:, lanes : 2 * lanes] = key_grad[...].astype(BF)
        out_ref[:, 2 * lanes :] = value_grad[...].astype(BF)
        grad_cols = dot(normed_ref[...], out_ref[...], ((0,), (0,))).astype(BF)
        split_store(kept_ref, away_ref, me_ref[0], grad_cols)
        bins = marks_ref.shape[1]
        wide = 3 * lanes
        notes = []
        for h in range(hp):
            total = jnp.zeros((1, bins), F32)
            for m in range(tiles):
                at = (tiles - 1 - m) * block
                x = bias_grad[h, :, at : at + block]
                x = jnp.concatenate([x, jnp.zeros((block, block), F32)], axis=1)
                half = block // 2
                while half >= 1:
                    x = x[:half] + pltpu.roll(x[half : 2 * half], 2 * block - half, 1)
                    half //= 2
                high, low = halves(x)
                part = marks_ref[m * 2 * block : (m + 1) * 2 * block, :]
                total += dot(high, part) + dot(low, part)
            notes.append(jnp.concatenate([total, jnp.zeros((1, wide - bins), F32)], axis=1))
        spot = lax.broadcasted_iota(jnp.int32, (1, AUX), 1) == me_ref[0]
        for h in range(hp):
            top = top_ref[h : h + 1, :]
            high = top.astype(BF).astype(F32)
            notes.append(
                jnp.concatenate(
                    [jnp.where(spot, high, 0.0), jnp.where(spot, top - high, 0.0)]
                    + [jnp.zeros((1, wide - 2 * AUX), F32)],
                    axis=1,
                )
            )
        notes.append(jnp.zeros((16 - 2 * hp, wide), F32))
        notes = jnp.concatenate(notes, axis=0).astype(BF)
        for ref in (kept_ref, away_ref):
            for at in range(ref.shape[0]):
                ref[at, ref.shape[1] - 16 :] = notes


def attend_back(me, attention_grad, weights, qkv, normed, marks, top, hp, block, spread):
    seq, lanes = attention_grad.shape
    count = seq // block
    width = normed.shape[1]
    tiles = weights.shape[3] // block
    fixed = lambda i: (0, 0)
    pairs = count * tiles * hp * block * block
    owned = (spread // 2, width // spread + 16, 3 * lanes)
    return call(
        lambda *refs: attend_back_kernel(tiles, hp, *refs),
        (struct((seq, 3 * lanes), BF), struct(owned, BF), struct(owned, BF)),
        60e9,
        10 * seq * lanes + 2 * pairs,
        grid=(count,),
        in_specs=[
            pl.BlockSpec(memory_space=pltpu.SMEM),
            pl.BlockSpec((block, lanes), lambda i: (i, 0)),
            pl.BlockSpec((1, hp, block, tiles * block), lambda i: (i, 0, 0, 0)),
            pl.BlockSpec((seq, 3 * lanes), fixed),
            pl.BlockSpec((seq, width), fixed),
            pl.BlockSpec(marks.shape, fixed),
            pl.BlockSpec(top.shape, fixed),
        ],
        out_specs=[pl.BlockSpec((seq, 3 * lanes), fixed)]
        + [pl.BlockSpec(owned, lambda i: (0, 0, 0))] * 2,
        scratch_shapes=[
            pltpu.VMEM((hp, block, tiles * block), F32),
            pltpu.VMEM((seq, lanes), F32),
            pltpu.VMEM((seq, lanes), F32),
        ],
    )(me, attention_grad, weights, qkv, normed, marks, top)


def upstream_kernel(places_ref, other_ref, grad_ref, out_ref):
    experts, capacity, _ = out_ref.shape
    rows = grad_ref.shape[0]
    slots = experts * capacity
    other = other_ref[...]
    slot = lax.broadcasted_iota(jnp.int32, (slots, rows), 0)
    first = jnp.where(slot == places_ref[0:1, :], 1.0, 0.0).astype(BF)
    second = jnp.where(slot == places_ref[1:2, :], 1.0, 0.0).astype(BF)
    sent = dot(first + second, grad_ref[...]).astype(BF)
    named = (dot(first, other[0]) + dot(second, other[1])).astype(BF)
    for at in range(experts):
        here = slice(at * capacity, (at + 1) * capacity)
        out_ref[at, :, 128:] = sent[here]
        out_ref[at, :, :128] = named[here]


def token_front_kernel(spread, me_ref, attn_ref, tok_ref, aux_ref, places_ref, *refs):
    w_refs = refs[:spread]
    attention_ref, resid_ref, normed_ref = refs[spread : spread + 3]
    buffers = refs[spread + 3 : -2]
    whole, arrived = refs[-2:]
    collect(w_refs, me_ref[0], whole, arrived)
    blocks = attn_ref.shape[0]
    attention = jnp.concatenate([attn_ref[at] for at in range(blocks)], axis=1)
    attention_ref[...] = attention
    width = attention.shape[1]
    gain = gain_row(aux_ref[...], 1)
    collected(w_refs, whole, arrived)
    resid = tok_ref[...].astype(F32) + dot(attention, whole[...].reshape(width, width))
    resid_ref[...] = resid
    r = lax.rsqrt(jnp.mean(resid * resid, axis=1, keepdims=True) + EPSILON)
    normed = (resid * r * gain).astype(BF)
    normed_ref[...] = normed
    slots = buffers[0].shape[0]
    slot = lax.broadcasted_iota(jnp.int32, (slots * len(buffers), normed.shape[0]), 0)
    named = (slot == places_ref[2:3, :]) | (slot == places_ref[3:4, :])
    sent = dot(jnp.where(named, 1.0, 0.0).astype(BF), normed).astype(BF)
    for k, buffer in enumerate(buffers):
        buffer[...] = sent[k * slots : (k + 1) * slots]


def token_middle_kernel(returned_ref, resid_ref, normed_ref, aux_ref, ids_ref, grad_ref,
                        mixed_ref, logit_ref, route_ref):
    slots = returned_ref.shape[0]
    rows = resid_ref.shape[0]
    slot = lax.broadcasted_iota(jnp.int32, (rows, slots), 1)
    first = jnp.where(slot == ids_ref[:, 0:1], 1.0, 0.0).astype(BF)
    second = jnp.where(slot == ids_ref[:, 1:2], 1.0, 0.0).astype(BF)
    returned = returned_ref[...]
    first_out = dot(first, returned)
    second_out = dot(second, returned)
    normed = normed_ref[...]
    logits = dot(normed, aux_ref[...])
    lane = lax.broadcasted_iota(jnp.int32, logits.shape, 1) - ROUTER_AT
    at_first = lane == ids_ref[:, 2:3]
    at_second = lane == ids_ref[:, 3:4]
    gap = jnp.sum(
        jnp.where(at_first, logits, 0.0) - jnp.where(at_second, logits, 0.0),
        axis=1, keepdims=True,
    )
    gate_one = 1.0 / (1.0 + jnp.exp(-gap))
    gate_two = 1.0 / (1.0 + jnp.exp(gap))
    mixed_ref[...] = (resid_ref[...] + gate_one * first_out + gate_two * second_out).astype(BF)
    upstream = grad_ref[...].astype(F32)
    change = jnp.sum(upstream * (first_out - second_out), axis=1, keepdims=True)
    slope = gate_one * gate_two * change
    logit = jnp.where(at_first, slope, 0.0) - jnp.where(at_second, slope, 0.0)
    logit_ref[...] = logit
    high, low = halves(logit)
    route_ref[...] = dot(normed, high, ((0,), (0,))) + dot(normed, low, ((0,), (0,)))


def norm_back(values, gain, grad):
    r = lax.rsqrt(jnp.mean(values * values, axis=1, keepdims=True) + EPSILON)
    scaled = grad * gain
    slope = jnp.mean(values * scaled, axis=1, keepdims=True)
    return r * scaled - values * (r * r * r * slope), r


def token_back_kernel(spread, me_ref, logit_ref, aux_ref, ids_ref, resid_ref, grad_ref, back_ref,
                      *refs):
    w_refs = refs[:spread]
    attention_ref, route_ref = refs[spread : spread + 2]
    resid_grad_ref, attention_grad_ref, kept_ref, away_ref, whole, arrived = refs[-6:]
    collect(w_refs, me_ref[0], whole, arrived)
    resid = resid_ref[...]
    rows, width = resid.shape
    slots = back_ref.shape[0]
    slot = lax.broadcasted_iota(jnp.int32, (rows, slots), 1)
    named = (slot == ids_ref[:, 0:1]) | (slot == ids_ref[:, 1:2])
    normed_grad = dot(jnp.where(named, 1.0, 0.0).astype(BF), back_ref[...])
    high, low = halves(logit_ref[...])
    aux = aux_ref[...]
    gain = gain_row(aux, 1)
    normed_grad += dot(high, aux, ((1,), (1,))) + dot(low, aux, ((1,), (1,)))
    part, r = norm_back(resid, gain, normed_grad)
    resid_grad = grad_ref[...].astype(F32) + part
    resid_grad_ref[...] = resid_grad
    gain_grad = jnp.sum(normed_grad * resid * r, axis=0, keepdims=True)
    proj = resid_grad.astype(BF)
    blocks, _, lanes = attention_grad_ref.shape
    collected(w_refs, whole, arrived)
    grad = dot(proj, whole[...].reshape(width, width), ((1,), (1,))).astype(BF)
    for at in range(blocks):
        attention_grad_ref[at] = grad[:, at * lanes : (at + 1) * lanes]
    grad_proj = dot(attention_ref[...], proj, ((0,), (0,))).astype(BF)
    lane = lax.broadcasted_iota(jnp.int32, (width, AUX), 1)
    gain_grad = jnp.broadcast_to(gain_grad, (AUX, width)).T
    small = jnp.where(lane == GAIN_AT, gain_grad, route_ref[...]).astype(BF)
    split_store(kept_ref, away_ref, me_ref[0], jnp.concatenate([grad_proj, small], axis=1))


def token_last_kernel(blocks_ref, w_ref, tok_ref, aux_ref, resid_grad_ref, out_ref, grads, total):
    part = pl.program_id(0)
    blocks, _, wide = blocks_ref.shape
    lanes = wide // 3
    for number in range(3):
        @pl.when(part == number)
        def _():
            for at in range(blocks):
                grads[:, at * lanes : (at + 1) * lanes] = blocks_ref[
                    at, :, number * lanes : (number + 1) * lanes
                ]

    term = dot(grads[...], w_ref[...], ((1,), (1,)))

    @pl.when(part == 0)
    def _():
        total[...] = term

    @pl.when(part > 0)
    def _():
        total[...] += term

    @pl.when(part == 2)
    def _():
        change, _ = norm_back(tok_ref[...].astype(F32), gain_row(aux_ref[...], 0), total[...])
        out_ref[...] = resid_grad_ref[...] + change


def note_row(notes, hp, spread, head):
    lane = lax.broadcasted_iota(jnp.int32, (1, AUX), 1)
    rel = jnp.where(lane < BUCKETS, notes[head : head + 1, :AUX], 0.0)
    tops = notes[hp + head : hp + head + 1]
    high = jnp.where(lane < spread, tops[:, :AUX], 0.0)
    low = jnp.where(lane < spread, tops[:, AUX : 2 * AUX], 0.0)
    return rel, high, low


def join_kernel(hp, spread, own_ref, proj_kept_ref, proj_got_ref, cols_kept_ref, cols_got_ref,
                kept_ref, away_ref):
    rows, wide = proj_kept_ref.shape
    pairs, own_rows, _ = kept_ref.shape
    even = own_ref[0] % 2 == 0
    proj = proj_kept_ref[...].astype(F32) + proj_got_ref[...].astype(F32)
    cols = cols_kept_ref[...].astype(F32) + cols_got_ref[...].astype(F32)
    notes = cols[rows:]
    row = lax.broadcasted_iota(jnp.int32, (own_rows, AUX), 0)
    extra = jnp.zeros((own_rows, AUX), F32)
    for h in range(hp):
        rel, high, low = note_row(notes, hp, spread, h)
        line = pltpu.roll(rel, BIAS_AT, 1) + pltpu.roll(high, TOP_AT, 1)
        line += pltpu.roll(low, TOP_LOW_AT, 1)
        extra += jnp.where(row == h + hp * (own_ref[0] % 2), line, 0.0)
    extra = jnp.concatenate([jnp.zeros((own_rows, wide - AUX), F32), extra], axis=1)
    for pair in range(pairs):
        at = 2 * pair * own_rows
        one, two = slice(at, at + own_rows), slice(at + own_rows, at + 2 * own_rows)
        kept_ref[pair, :, :wide] = (jnp.where(even, proj[one], proj[two]) + extra).astype(BF)
        away_ref[pair, :, :wide] = (jnp.where(even, proj[two], proj[one]) + extra).astype(BF)
        kept_ref[pair, :, wide:] = jnp.where(even, cols[one], cols[two]).astype(BF)
        away_ref[pair, :, wide:] = jnp.where(even, cols[two], cols[one]).astype(BF)


def pair_kernel(wide, own_ref, kept_ref, got_ref, *sends):
    even = own_ref[0] % 2 == 0
    for k, send in enumerate(sends):
        pair = (own_ref[0] // 2) ^ k
        kept, got = kept_ref[pair], got_ref[pair]
        send[:, :wide] = (kept[:, :wide].astype(F32) + got[:, :wide].astype(F32)).astype(BF)
        columns = kept.shape[1] - wide
        send[:, wide : wide + columns] = jnp.where(even, kept[:, wide:], got[:, wide:])
        send[:, wide + columns :] = jnp.where(even, got[:, wide:], kept[:, wide:])


def join_plain(hp, spread, place, groups, proj_terms, cols_terms):
    proj, cols = joined(proj_terms), joined(cols_terms)
    rows, wide = proj.shape
    own_rows = rows // groups
    notes = cols[rows:]
    whole = jnp.concatenate([proj, cols[:rows]], axis=1).reshape(groups, own_rows, -1)
    lines = []
    for h in range(hp):
        rel, high, low = note_row(notes, hp, spread, h)
        line = jnp.roll(rel, BIAS_AT, 1) + jnp.roll(high, TOP_AT, 1) + jnp.roll(low, TOP_LOW_AT, 1)
        lines.append(line)
    extra = jnp.concatenate(lines, axis=0)
    extra = jnp.pad(extra, ((0, own_rows - hp), (wide - AUX, whole.shape[2] - wide)))
    whole = (whole + extra).astype(BF)
    return [
        lax.dynamic_index_in_dim(whole, place ^ k, axis=0, keepdims=False) for k in range(groups)
    ]


def owner_kernel(hp, sharers, spread, own_ref, q_ref, k_ref, v_ref, gain_ref, *refs):
    (proj_ref, route_ref, gain_two_ref, gq_ref, gk_ref, gv_ref, gain_one_ref, rel_ref,
     factor_ref, summary_ref) = refs[-10:]
    blocks = refs[:-10]
    experts = route_ref.shape[0]
    eye = lax.broadcasted_iota(jnp.int32, (proj_ref.shape[0],) * 2, 0)
    eye = eye == lax.broadcasted_iota(jnp.int32, eye.shape, 1)

    def as_row(column):
        return jnp.sum(jnp.where(eye, column, 0.0), axis=0, keepdims=True)

    width = proj_ref.shape[1]
    lanes = hp * HDIM
    sources = (blocks[0].shape[1] - width - AUX) // (3 * lanes)
    total = None
    for block in blocks:
        term = block[:, : width + AUX].astype(F32)
        total = term if total is None else total + term
    proj_ref[...] = total[:, :width]
    small = total[:, width:].T
    route_ref[...] = small[ROUTER_AT : ROUTER_AT + experts]
    gain_two_ref[...] = small[GAIN_AT : GAIN_AT + 1]
    outs = (gq_ref, gk_ref, gv_ref)
    for out in outs:
        out[...] = jnp.zeros_like(out)
    lane = lax.broadcasted_iota(jnp.int32, (1, 128), 1)
    summary_ref[...] = jnp.where(
        lax.broadcasted_iota(jnp.int32, summary_ref.shape, 1) == 64, MASKED, 0.0
    )
    for k, source in [(k, source) for k in range(len(blocks)) for source in range(sources)]:
        block = blocks[k]
        seat = (((own_ref[0] // sources) ^ k) * sources + source) % sharers
        at = pl.multiple_of(seat * lanes, lanes)
        for part, out in enumerate(outs):
            first = width + AUX + (3 * source + part) * lanes
            out[:, pl.ds(at, lanes)] += block[:, first : first + lanes].astype(F32)
        notes = block[:, width : width + AUX].astype(F32)
        for h in range(hp):
            note = notes[source * hp + h : source * hp + h + 1]
            rel = jnp.where(lane < BUCKETS, pltpu.roll(note, AUX - BIAS_AT, 1), 0.0)
            tops = pltpu.roll(note, AUX - TOP_AT, 1) + pltpu.roll(note, AUX - TOP_LOW_AT, 1)
            top = jnp.max(jnp.where(lane < spread, tops, MASKED), axis=1, keepdims=True)
            old = summary_ref[pl.ds(seat * hp + h, 1), :]
            new = jnp.where(lane == 64, jnp.maximum(old, top), old + rel)
            summary_ref[pl.ds(seat * hp + h, 1), :] = new
    rel_ref[...] = summary_ref[:, :BUCKETS]
    factor_ref[...] = jnp.sqrt(CLIP_LEVEL / jnp.maximum(summary_ref[...].T[64:65], 1.0))
    grad = jnp.zeros((proj_ref.shape[0], 1), F32)
    for out, w_ref in zip(outs, (q_ref, k_ref, v_ref)):
        grad += jnp.sum(out[...] * w_ref[...].astype(F32), axis=1, keepdims=True)
    gain_one_ref[...] = as_row(grad) / gain_ref[...]


GELU_A = 0.7978845608028654
GELU_B = 0.044715


def expert_kernel(groups, own_ref, upstream_ref, aux_ref, gate_ref, up_ref, down_ref, *refs):
    blocks = refs[:groups]
    (gate_pre_ref, up_pre_ref, out_ref, rows_ref, slot_grad_ref, grad_down_ref, total) = refs[groups:]
    f = pl.program_id(0)
    capacity, width = blocks[0].shape

    @pl.when(f == 0)
    def _():
        total[...] = jnp.zeros_like(total)
        for k, block in enumerate(blocks):
            rows_ref[k * capacity : (k + 1) * capacity, :] = block[...]
        all_logits = dot(rows_ref[...], aux_ref[...])
        for k in range(groups):
            here = slice(k * capacity, (k + 1) * capacity)
            logits = all_logits[here]
            lane = lax.broadcasted_iota(jnp.int32, logits.shape, 1) - ROUTER_AT
            upstream = upstream_ref[own_ref[0] ^ k]
            other = upstream[:, 0:1].astype(F32).astype(jnp.int32)
            gap = jnp.sum(
                jnp.where(lane == other, logits, 0.0) - jnp.where(lane == own_ref[0], logits, 0.0),
                axis=1, keepdims=True,
            )
            gate = 1.0 / (1.0 + jnp.exp(gap))
            slot_grad_ref[here, :] = (gate * upstream[:, 128:].astype(F32)).astype(BF)

    rows = rows_ref[...]
    gate_pre = dot(rows, gate_ref[...])
    up_pre = dot(rows, up_ref[...])
    gate_pre_ref[...] = gate_pre
    up_pre_ref[...] = up_pre
    inner = jnp.tanh(GELU_A * (gate_pre + GELU_B * gate_pre * gate_pre * gate_pre))
    hidden = (0.5 * gate_pre * (1.0 + inner) * up_pre).astype(BF)
    total[...] += dot(hidden, down_ref[...])
    grad_down_ref[...] = dot(hidden, slot_grad_ref[...], ((0,), (0,))).astype(BF)

    @pl.when(f == pl.num_programs(0) - 1)
    def _():
        for k in range(groups):
            out_ref[own_ref[0] ^ k] = total[k * capacity : (k + 1) * capacity, :].astype(BF)


def expert_forward(own, upstream, aux, blocks, gate, up, down, tile):
    groups = len(blocks)
    capacity, width = blocks[0].shape
    count = groups * capacity
    ff = gate.shape[1]
    fixed = lambda f: (0, 0)
    cols = lambda f: (0, f)
    return call(
        lambda *refs: expert_kernel(groups, *refs),
        (
            struct((count, ff), F32),
            struct((count, ff), F32),
            struct((groups, capacity, width), BF),
            struct((count, width), BF),
            struct((count, width), BF),
            struct((ff, width), BF),
        ),
        24e9,
        6 * width * ff + 10 * count * ff,
        grid=(ff // tile,),
        in_specs=[
            pl.BlockSpec(memory_space=pltpu.SMEM),
            pl.BlockSpec(upstream.shape, lambda f: (0, 0, 0)),
            pl.BlockSpec(aux.shape, fixed),
            pl.BlockSpec((width, tile), cols),
            pl.BlockSpec((width, tile), cols),
            pl.BlockSpec((tile, width), lambda f: (f, 0)),
        ]
        + [pl.BlockSpec((capacity, width), fixed)] * groups,
        out_specs=[
            pl.BlockSpec((count, tile), cols),
            pl.BlockSpec((count, tile), cols),
            pl.BlockSpec((groups, capacity, width), lambda f: (0, 0, 0)),
            pl.BlockSpec((count, width), fixed),
            pl.BlockSpec((count, width), fixed),
            pl.BlockSpec((tile, width), lambda f: (f, 0)),
        ],
        scratch_shapes=[pltpu.VMEM((count, width), F32)],
    )(own, upstream, aux, gate, up, down, *blocks)


def split_store(kept_ref, away_ref, me, values):
    rows = values.shape[0] // (2 * kept_ref.shape[0])
    for d in range(2 * kept_ref.shape[0]):
        block = values[d * rows : (d + 1) * rows]
        @pl.when(me % 2 == d % 2)
        def _():
            kept_ref[d // 2, :rows] = block

        @pl.when(me % 2 != d % 2)
        def _():
            away_ref[d // 2, :rows] = block


def expert_back_kernel(own_ref, me_ref, slot_grad_ref, rows_ref, gate_pre_ref, up_pre_ref, down_ref,
                       gate_ref, up_ref, row_grad_ref, grad_gate_ref, up_kept_ref, up_away_ref,
                       total, pre_grads, split_rows):
    f = pl.program_id(0)
    tiles = pl.num_programs(0) - 1
    tile = gate_ref.shape[1]
    groups, capacity, _ = row_grad_ref.shape

    def through_gelu(slot):
        hidden_grad = dot(slot_grad_ref[...], down_ref[...], ((1,), (1,)))
        v = gate_pre_ref[...]
        square = v * v
        inner = jnp.tanh(v * (GELU_A + GELU_A * GELU_B * square))
        half = 0.5 + 0.5 * inner
        slope = half + (0.5 * v) * (1.0 - inner * inner) * (
            GELU_A + 3.0 * GELU_A * GELU_B * square
        )
        pre_grads[slot, :, :tile] = (hidden_grad * up_pre_ref[...] * slope).astype(BF)
        pre_grads[slot, :, tile:] = (hidden_grad * (v * half)).astype(BF)

    def to_weights(slot):
        both = pre_grads[slot]
        weights = jnp.concatenate([gate_ref[...], up_ref[...]], axis=1)
        total[...] += dot(both, weights, ((1,), (1,)))
        grad_gate_ref[...] = dot(rows_ref[...], both[:, :tile], ((0,), (0,))).astype(BF)
        grads = dot(split_rows[...], both[:, tile:], ((0,), (0,))).astype(BF)
        half = grads.shape[0] // 2
        up_kept_ref[...] = grads[:half].reshape(up_kept_ref.shape)
        up_away_ref[...] = grads[half:].reshape(up_kept_ref.shape)

    @pl.when(f == 0)
    def _():
        total[...] = jnp.zeros_like(total)
        part = up_kept_ref.shape[1]
        half = rows_ref.shape[1] // 2
        even = me_ref[0] % 2 == 0
        for pair in range(up_kept_ref.shape[0]):
            one = rows_ref[:, 2 * pair * part : (2 * pair + 1) * part]
            two = rows_ref[:, (2 * pair + 1) * part : (2 * pair + 2) * part]
            at = pair * part
            split_rows[:, at : at + part] = jnp.where(even, one, two)
            split_rows[:, half + at : half + at + part] = jnp.where(even, two, one)
        through_gelu(0)

    @pl.when((f > 0) & (f < tiles))
    def _():
        to_weights((f - 1) % 2)
        through_gelu(f % 2)

    @pl.when(f == tiles)
    def _():
        to_weights((f - 1) % 2)
        for k in range(groups):
            row_grad_ref[own_ref[0] ^ k] = total[k * capacity : (k + 1) * capacity, :].astype(BF)


def expert_backward(own, me, slot_grad, rows, gate_pre, up_pre, gate, up, down, tile, groups,
                    spread):
    count, width = rows.shape
    ff = gate.shape[1]
    tiles = ff // tile
    fixed = lambda f: (0, 0)
    now = lambda f: (0, jnp.minimum(f, tiles - 1))
    before = lambda f: (0, jnp.maximum(f - 1, 0))
    owned = (spread // 2, width // spread)
    return call(
        expert_back_kernel,
        [
            struct((groups, count // groups, width), BF),
            struct((width, ff), BF),
        ]
        + [struct(owned + (ff,), BF)] * 2,
        30e9,
        12 * width * ff + 10 * count * ff,
        grid=(tiles + 1,),
        in_specs=[
            pl.BlockSpec(memory_space=pltpu.SMEM),
            pl.BlockSpec(memory_space=pltpu.SMEM),
            pl.BlockSpec((count, width), fixed),
            pl.BlockSpec((count, width), fixed),
            pl.BlockSpec((count, tile), now),
            pl.BlockSpec((count, tile), now),
            pl.BlockSpec((tile, width), lambda f: (jnp.minimum(f, tiles - 1), 0)),
            pl.BlockSpec((width, tile), before),
            pl.BlockSpec((width, tile), before),
        ],
        out_specs=[
            pl.BlockSpec((groups, count // groups, width), lambda f: (0, 0, 0)),
            pl.BlockSpec((width, tile), before),
        ]
        + [pl.BlockSpec(owned + (tile,), lambda f: (0, 0, jnp.maximum(f - 1, 0)))] * 2,
        scratch_shapes=[
            pltpu.VMEM((count, width), F32),
            pltpu.VMEM((2, count, 2 * tile), BF),
            pltpu.VMEM((count, width), BF),
        ],
    )(own, me, slot_grad, rows, gate_pre, up_pre, down, gate, up)


def slot_places(routes, experts, capacity):
    chosen = (routes[:, :, None] == jnp.arange(experts, dtype=jnp.int32)[None, None, :]).astype(
        jnp.int32
    )
    order = jnp.swapaxes(chosen, 0, 1).reshape(-1, experts)
    before = jnp.cumsum(order, axis=0) - order
    slots = jnp.sum(before * order, axis=1).reshape(TOP, -1).T
    return routes * capacity + slots


def flip(values, axis, mask):
    n = lax.axis_size(axis)
    return lax.ppermute(values, axis, [(k, k ^ mask) for k in range(n)])


def gather_parts(part, axis):
    return gather_rest({0: part}, axis, lax.axis_size(axis) // 2)


def gather_rest(held, axis, bit):
    while bit >= 1:
        held.update({j ^ bit: flip(values, axis, bit) for j, values in list(held.items())})
        bit //= 2
    return [held[j] for j in range(len(held))]


def swap_parts(parts, axis):
    return [parts[0]] + [flip(parts[k], axis, k) for k in range(1, len(parts))]


def ring_parts(tokens, before, between):
    devices = lax.axis_size("expert")
    line = list(range(0, devices, 2)) + list(range(devices - 1, 0, -2))
    spots = [line.index(k) for k in range(devices)]

    def move(values, step):
        pairs = [(line[k], line[(k + step) % devices]) for k in range(devices)]
        return lax.ppermute(values, "expert", pairs)

    ahead = [tokens]
    behind = [tokens]
    half = devices // 2
    for k in range(1, half):
        pair = (move(ahead[-1], 1), move(behind[-1], -1))
        if k == half - 2:
            *pair, first = lax.optimization_barrier((*pair, before[0]))
            before = (between(first),) + before[1:]
        elif k == half - 1:
            *pair, before = lax.optimization_barrier((*pair, before))
        else:
            pair = lax.optimization_barrier(pair)
        ahead.append(pair[0])
        behind.append(pair[1])
    cut = tokens.shape[0] // 2
    farthest = (move(ahead[-1][:cut], 1), move(behind[-1][cut:], -1))
    parts = ahead + behind[:0:-1] + list(farthest)
    spot = jnp.asarray(spots, jnp.int32)
    mine = jnp.sum(jnp.where(jnp.arange(devices) == lax.axis_index("expert"), spot, 0))
    gap = (mine - spot) % devices
    gap = jnp.where(gap == half, devices - 1, jnp.where(gap > half, gap - 1, gap))
    return gap.astype(jnp.int32), parts, before


def scatter_step(parts, axis, me, bit):
    pairs = parts.reshape((parts.shape[0] // 2, 2) + parts.shape[1:])
    mine = (me // bit) % 2
    away = lax.dynamic_index_in_dim(pairs, 1 - mine, axis=1, keepdims=False)
    kept = lax.dynamic_index_in_dim(pairs, mine, axis=1, keepdims=False)
    return kept, flip(away, axis, bit)


def joined(parts):
    return parts[0].astype(F32) + parts[1].astype(F32)


def scatter_rest(parts, axis):
    n = lax.axis_size(axis)
    me = lax.axis_index(axis)
    bit = 2
    while True:
        terms = scatter_step(parts, axis, me, bit)
        bit *= 2
        if bit >= n:
            return tuple(term[0] for term in terms)
        parts = joined(terms).astype(BF)


def body(tokens, gain_attn, w_query, w_key, w_value, w_output, rel_bias, gain_ffn, w_router,
         expert_gate, expert_up, expert_down, routes, doc_lengths, seq_valid, grad_output):
    length, width = tokens.shape
    groups = lax.axis_size("expert")
    spread = lax.axis_size("dp")
    place = lax.axis_index("expert")
    device = lax.axis_index("dp") * groups + place
    experts = w_router.shape[1]
    capacity = 5 * TOP * length // (4 * experts)
    slots = experts * capacity
    sharers = SEQ // length
    hp = HEADS // sharers
    lanes = hp * HDIM
    own_rows = w_query.shape[0]
    teams = None
    if groups != sharers:
        teams = [list(range(at, at + sharers)) for at in range(0, groups, sharers)]
    both = ("dp", "expert")

    def exchange(blocks):
        return lax.all_to_all(blocks, "expert", 0, 0, axis_index_groups=teams, tiled=True)

    def exchange_all(blocks):
        return lax.all_to_all(blocks, "expert", 0, 0, tiled=True)

    def columns(w):
        return w.reshape(own_rows, sharers, lanes).swapaxes(0, 1)

    extra = jnp.concatenate([gain_attn[:, None], gain_ffn[:, None], w_router], axis=1)
    extra = jnp.pad(extra, ((0, 0), (0, AUX - extra.shape[1])))
    sent = jnp.concatenate(
        [
            columns(w_query),
            columns(w_key),
            columns(w_value),
            jnp.broadcast_to(extra[None], (sharers, own_rows, AUX)),
        ],
        axis=2,
    )
    sent = jnp.tile(sent, (groups // sharers, 1, 1))
    gate_all = lax.all_gather(expert_gate[0], "dp", axis=0, tiled=True)
    up_all = lax.all_gather(expert_up[0], "dp", axis=0, tiled=True)
    down_all = lax.all_gather(expert_down[0], "dp", axis=0, tiled=True)

    places = slot_places(routes, experts, capacity)
    near_places = places + ((routes ^ place) - routes) * capacity
    ids = jnp.concatenate([places, routes, near_places], axis=1)
    ids = jnp.pad(ids, ((0, 0), (0, 128 - ids.shape[1])))
    places_row = jnp.pad(
        jnp.concatenate([places, near_places], axis=1).T, ((0, 4), (0, 0)), constant_values=-1
    )
    other = jnp.broadcast_to(routes.T[::-1, :, None], (TOP, length, 128)).astype(BF)
    upstream = call(
        upstream_kernel,
        struct((experts, capacity, width + 128), BF),
        3e9,
        4 * slots * width,
    )(places_row, other, grad_output)

    number = (device * length) // SEQ
    ends = jnp.cumsum(lax.dynamic_index_in_dim(doc_lengths, number, keepdims=False))
    ends = jnp.concatenate([ends, lax.dynamic_index_in_dim(seq_valid, number)]).astype(jnp.int32)
    block = length
    marks, inside = diagonal_tables(block, WINDOW, BUCKETS)
    head_at = (place % sharers) * hp
    own_bias = lax.dynamic_slice_in_dim(rel_bias, head_at, hp, axis=1)
    diag = jnp.dot(jnp.asarray(marks), own_bias, precision=lax.Precision.HIGHEST)
    diag = jnp.where(jnp.asarray(inside)[:, None], diag, MASKED)
    tiles = WINDOW // block + 1
    diag = diag.T.reshape(hp * tiles, 2 * block)
    packed = exchange_all(sent).reshape(groups * own_rows, 3 * lanes + AUX)
    mixed_rows = jnp.concatenate([tokens, w_output, w_query, w_key, w_value], axis=0)
    if teams is None:
        def between(values):
            return gather_parts(values, "dp")

        before = (packed, upstream, diag, ends, ids)
        pick, parts, before = ring_parts(mixed_rows, before, between)
        packed, upstream, diag, ends, ids = before
    else:
        whole = lax.all_gather(mixed_rows, "expert", axis=0, axis_index_groups=teams)
        pick = jnp.arange(sharers, dtype=jnp.int32)
        parts = [whole[at] for at in range(sharers)]
        packed = gather_parts(packed, "dp")
    me = lax.axis_index("dp").astype(jnp.int32).reshape(1)
    if teams is None:
        output_rows, qkv_rows = call(
            lambda *refs: output_rows_kernel(len(parts), length, own_rows, *refs),
            (struct((groups * own_rows, width), BF), struct((groups * own_rows, 3 * width), BF)),
            1e9,
            16 * groups * own_rows * width,
            mib=12, in_specs=[pl.BlockSpec(memory_space=pltpu.SMEM)]
            + [pl.BlockSpec(memory_space=pl.ANY)] * len(parts),
            out_specs=[pl.BlockSpec(memory_space=pltpu.VMEM)] * 2,
            scratch_shapes=[pltpu.SemaphoreType.DMA((sharers, 4))],
        )(pick, *parts)
        output_rows, attend_parts = lax.optimization_barrier((output_rows, parts))
    else:
        output_rows = lax.all_gather(w_output, "expert", axis=0, tiled=True)
        qkv_rows = jnp.concatenate([w_query, w_key, w_value], axis=1)
        qkv_rows = lax.all_gather(qkv_rows, "expert", axis=0, tiled=True)
        attend_parts = parts
    output_parts = {0: output_rows, spread // 2: flip(output_rows, "dp", spread // 2)}

    upstream, _ = lax.optimization_barrier((upstream, parts))
    upstream = exchange_all(upstream)

    normed_one, qkv, weights, attn, top, aux = attend(
        pick, me, attend_parts, packed, diag, ends, hp, block
    )
    attn, upstream, output_parts = lax.optimization_barrier((attn, upstream, output_parts))
    output_parts = gather_rest(output_parts, "dp", spread // 4)
    attn_blocks = exchange(attn.reshape(sharers, length, lanes))

    vmem = pl.BlockSpec(memory_space=pltpu.VMEM)
    smem = pl.BlockSpec(memory_space=pltpu.SMEM)
    loose = pl.BlockSpec(memory_space=pl.ANY)
    gathered = [
        pltpu.VMEM((spread,) + output_parts[0].shape, BF),
        pltpu.SemaphoreType.DMA((spread,)),
    ]
    attention, resid, normed_two, *buffers = call(
        lambda *refs: token_front_kernel(spread, *refs),
        [
            struct((length, width), BF),
            struct((length, width), F32),
            struct((length, width), BF),
        ]
        + [struct((capacity, width), BF)] * groups,
        5e9,
        2 * width * width + 8 * length * width,
        mib=24, in_specs=[smem] + [vmem] * 4 + [loose] * spread,
        scratch_shapes=gathered,
    )(me, attn_blocks, tokens, aux, places_row, *output_parts)
    rows = swap_parts(buffers, "expert")
    qkv_rows, _ = lax.optimization_barrier((qkv_rows, attn))
    qkv_all = lax.all_gather(qkv_rows, "dp", axis=0, tiled=True)

    tile = 256 if expert_gate.shape[2] % 256 == 0 else 128
    own = place.astype(jnp.int32).reshape(1)
    gate_pre, up_pre, expert_out, rows, slot_grad, grad_down = expert_forward(
        own, upstream, aux, rows, gate_all, up_all, down_all, tile
    )
    expert_out, qkv_all = lax.optimization_barrier((expert_out, qkv_all))
    returned = exchange_all(expert_out)
    row_grad, *expert_grads = expert_backward(
        own, me, slot_grad, rows, gate_pre, up_pre, gate_all, up_all, down_all, tile, groups,
        spread,
    )
    returned, row_grad, expert_grads = lax.optimization_barrier(
        (returned, row_grad, expert_grads)
    )
    grad_gate, up_kept, up_away = expert_grads
    up_first = joined((up_kept, flip(up_away, "dp", 1))).astype(BF)
    owned_down = lax.psum_scatter(grad_down, "dp", scatter_dimension=0, tiled=True)
    returned = returned.reshape(slots, width)
    back = exchange_all(row_grad)
    mixed, logit_grad, route_grad = call(
        token_middle_kernel,
        (
            struct((length, width), BF),
            struct((length, 128), F32),
            struct((width, 128), F32),
        ),
        5e9,
        2 * slots * width + 8 * length * width,
    )(returned, resid, normed_two, aux, ids, grad_output)
    back, owned_down = lax.optimization_barrier((back, owned_down))
    owned_down = owned_down.astype(F32)
    back = back.reshape(slots, width)
    cores = [list(range(core, spread, 2)) for core in range(2)]

    def scatter_chips(parts):
        parts = parts.reshape((-1,) + parts.shape[2:])
        return lax.psum_scatter(
            parts, "dp", scatter_dimension=0, axis_index_groups=cores, tiled=True
        )

    owned_gate = lax.psum_scatter(grad_gate, "dp", scatter_dimension=0, tiled=True)
    owned_up = scatter_chips(up_first)
    resid_grad, attention_grad, proj_kept, proj_away = call(
        lambda *refs: token_back_kernel(spread, *refs),
        (
            struct((length, width), F32),
            struct((sharers, length, lanes), BF),
            struct((spread // 2, width // spread, width + AUX), BF),
            struct((spread // 2, width // spread, width + AUX), BF),
        ),
        6e9,
        2 * width * width + 2 * slots * width + 8 * length * width,
        in_specs=[smem] + [vmem] * 6 + [loose] * spread + [vmem] * 2,
        scratch_shapes=gathered,
    )(me, logit_grad, aux, ids, resid, grad_output, back, *output_parts, attention, route_grad)
    attention_grad = exchange(attention_grad).reshape(SEQ, lanes)
    proj_first = proj_kept.astype(F32) + flip(proj_away, "dp", 1).astype(F32)
    attention_grad, proj_first, _ = lax.optimization_barrier(
        (attention_grad, proj_first.astype(BF), up_first)
    )
    proj_terms = scatter_rest(proj_first, "dp")

    grad_qkv_rows, cols_kept, cols_away = attend_back(
        me, attention_grad, weights, qkv, normed_one, jnp.asarray(marks, BF), top, hp, block, spread
    )
    grad_qkv_rows, cols_away, proj_terms, owned_gate = lax.optimization_barrier(
        (grad_qkv_rows, cols_away, proj_terms, owned_gate)
    )
    grads_here = exchange(grad_qkv_rows.reshape(sharers, length, 3 * lanes))
    owned_gate = owned_gate.astype(F32)
    fixed = lambda part: (0, 0)
    grad_tokens = call(
        token_last_kernel,
        struct((length, width), F32),
        60e9,
        6 * width * width + 12 * length * width,
        grid=(3,),
        mib=24, in_specs=[
            pl.BlockSpec(grads_here.shape, lambda part: (0, 0, 0)),
            pl.BlockSpec((width, width), lambda part: (0, part)),
            pl.BlockSpec((length, width), fixed),
            pl.BlockSpec(aux.shape, fixed),
            pl.BlockSpec((length, width), fixed),
        ],
        out_specs=pl.BlockSpec((length, width), fixed),
        scratch_shapes=[pltpu.VMEM((length, width), BF), pltpu.VMEM((length, width), F32)],
    )(grads_here, qkv_all, tokens, aux, resid_grad)

    cols_first = cols_kept.astype(F32) + flip(cols_away, "dp", 1).astype(F32)
    cols_terms = scatter_rest(cols_first.astype(BF), "dp")
    if own_rows % 16 == 0:
        pairs = groups // 2
        blocks = struct((pairs, own_rows, width + AUX + 3 * lanes), BF)
        pairs_kept, pairs_away = call(
            lambda *refs: join_kernel(hp, spread, *refs),
            [blocks] * 2,
            1e9,
            8 * groups * own_rows * width,
            mib=12, in_specs=[smem] + [vmem] * 4,
        )(own, *proj_terms, *cols_terms)
        sends = call(
            lambda *refs: pair_kernel(width + AUX, *refs),
            [struct((own_rows, width + AUX + 6 * lanes), BF)] * pairs,
            1e9,
            8 * groups * own_rows * width,
            mib=12, in_specs=[smem] + [vmem] * 2,
        )(own, pairs_kept, flip(pairs_away, "expert", 1))
        owned = [sends[0]] + [flip(sends[k], "expert", 2 * k) for k in range(1, pairs)]
    else:
        sends = join_plain(hp, spread, place, groups, proj_terms, cols_terms)
        owned = swap_parts(sends, "expert")
    grad_tokens, owned_up = lax.optimization_barrier((grad_tokens, owned_up))
    owned_up = owned_up.astype(F32)
    *owned, grad_tokens = lax.optimization_barrier((*owned, grad_tokens))
    grad_proj, route, gain_two, grad_q, grad_k, grad_v, gain_one, rel, factor = call(
        lambda *refs: owner_kernel(hp, sharers, spread, *refs),
        (
            struct((own_rows, width), F32),
            struct((experts, own_rows), F32),
            struct((1, own_rows), F32),
            struct((own_rows, width), F32),
            struct((own_rows, width), F32),
            struct((own_rows, width), F32),
            struct((1, own_rows), F32),
            struct((HEADS, BUCKETS), F32),
            struct((1, HEADS), F32),
        ),
        2e9,
        8 * own_rows * width,
        mib=12, in_specs=[smem] + [vmem] * (4 + len(owned)),
        scratch_shapes=[pltpu.VMEM((HEADS, 128), F32)],
    )(own, w_query, w_key, w_value, gain_attn.astype(F32)[None], *owned)
    return (
        mixed,
        grad_tokens,
        gain_one[0],
        grad_q,
        grad_k,
        grad_v,
        grad_proj,
        rel.T,
        gain_two[0],
        route.T,
        owned_gate[None],
        owned_up[None],
        owned_down[None],
        factor[0],
    )


def solution(mesh):
    rows = P(("dp", "expert"), None)
    vector = P(("dp", "expert"))
    expert = P("expert", "dp", None)
    return jax.shard_map(
        body,
        mesh=mesh,
        in_specs=(
            rows, vector, rows, rows, rows, rows, P(), vector, rows,
            expert, expert, expert, rows, P(), P(), rows,
        ),
        out_specs=(
            rows, rows, vector, rows, rows, rows, rows, P(), vector, rows,
            expert, expert, expert, P(),
        ),
        check_vma=False,
    )
```

profile of v0, /device:TPU:4, one launch (start us, length us, event | category | flops | bytes accessed | tf_op | source)
XLA Modules:
  0.0 389.8 jit_solution(11381700314835720166)
XLA Ops:
  12.0 17.1 %collective-permute-done.refs_2_.refs_3_ = bf16[384,1024]{1,0:T(8,128)(2,1)S(1)} collective-permute-done((bf16[384,1024]{1,0:T(8,128)(2,1)S(1)}, bf16[384,1024]{1,0:T(8,128)(2,1)S(1)}, u32[]{:S(2)}, u32[]{:S(2)}) %collective-permute-start) | collective-permute-done | bytes 786464 | tf_op jit(solution)/shard_map/ppermute | solution.py:915
  31.9 6.6 %all-to-all-start = ((bf16[8,32,512]{2,1,0:T(8,128)(2,1)}), bf16[8,32,512]{2,1,0:T(8,128)(2,1)S(1)}, u32[]{:S(2)}, u32[]{:S(2)}) async-start(bf16[8,32,512]{2,1,0:T(8,128)(2,1)} %pad_maximum_fusion), calls=%async_computation | async-start | bytes 524288 | tf_op jit(solution)/shard_map/all_to_all | solution.py:988
  42.5 13.6 %all-to-all-done = bf16[8,32,512]{2,1,0:T(8,128)(2,1)S(1)} async-done(((bf16[8,32,512]{2,1,0:T(8,128)(2,1)}), bf16[8,32,512]{2,1,0:T(8,128)(2,1)S(1)}, u32[]{:S(2)}, u32[]{:S(2)}) %all-to-all-start) | async-done | bytes 262176 | tf_op jit(solution)/shard_map/all_to_all | solution.py:988
  76.0 5.7 %collective-permute-done.10.refs_9_.refs_10_ = bf16[192,1024]{1,0:T(8,128)(2,1)S(1)} collective-permute-done((bf16[192,1024]{1,0:T(8,128)(2,1)S(1)}, bf16[192,1024]{1,0:T(8,128)(2,1)S(1)}, u32[]{:S(2)}, u32[]{:S(2)}) %collective-permute-start.10) | collective-permute-done | bytes 393248 | tf_op jit(solution)/shard_map/ppermute | solution.py:915
  83.6 5.1 %all-to-all-start.1 = ((bf16[8,80,1152]{2,1,0:T(8,128)(2,1)}), bf16[8,80,1152]{2,1,0:T(8,128)(2,1)}, u32[]{:S(2)}, u32[]{:S(2)}) async-start(bf16[8,80,1152]{2,1,0:T(8,128)(2,1)} %shard_map.299), calls=%async_computation.1 | async-start | bytes 2949120 | tf_op jit(solution)/shard_map/all_to_all | solution.py:988
  98.8 23.1 %shard_map.301 = (bf16[2048,1024]{1,0:T(8,128)(2,1)}, bf16[2048,384]{1,0:T(8,128)(2,1)}, bf16[8,2,256,1280]{3,2,1,0:T(8,128)(2,1)}, bf16[2048,128]{1,0:T(8,128)(...) custom-call(s32[8]{0:T(128)} %copy-done.22, s32[1]{0:T(128)} %bitcast.1.refs_1_.refs_0_.me_ref, ...), custom_call_target="tpu_custom_call" | custom-call | flops 24000000000 | bytes 27262976 | tf_op jit(solution)/shard_map/pallas_call | solution.py:230
  122.0 6.0 %all-to-all-start.2 = ((bf16[8,256,128]{2,1,0:T(8,128)(2,1)}), bf16[8,256,128]{2,1,0:T(8,128)(2,1)S(1)}, u32[]{:S(2)}, u32[]{:S(2)}) async-start(bf16[8,256,128]{2,1,0:T(8,128)(2,1)} %bitcast.18), calls=%async_computation.2 | async-start | bytes 1048576 | tf_op jit(solution)/shard_map/all_to_all | solution.py:985
  131.0 6.7 %all-to-all-done.2.refs_1_ = bf16[8,256,128]{2,1,0:T(8,128)(2,1)S(1)} async-done(((bf16[8,256,128]{2,1,0:T(8,128)(2,1)}), bf16[8,256,128]{2,1,0:T(8,128)(2,1)S(1)}, u32[]{:S(2)}, u32[]{:S(2)}) %all-to-all-start.2) | async-done | bytes 524320 | tf_op jit(solution)/shard_map/all_to_all | solution.py:985
  152.0 6.1 %collective-permute-start.20 = (bf16[80,1024]{1,0:T(8,128)(2,1)S(1)}, bf16[80,1024]{1,0:T(8,128)(2,1)S(1)}, u32[]{:S(2)}, u32[]{:S(2)}) collective-permute-start(bf16[80,1024]{1,0:T(8,128)(2,1)S(1)} %get-tuple-element.161), channel_id=1, source_target_pairs={{0,7},{1,6},{2,5},{3,4},{4,3},{5,2},{6,1},{7,0},{8,15},{9,14},{10,... | collective-permute-start | bytes 491528 | tf_op jit(solution)/shard_map/ppermute | solution.py:890
  158.2 6.1 %collective-permute-done.17.refs_10_ = bf16[80,1024]{1,0:T(8,128)(2,1)S(1)} collective-permute-done((bf16[80,1024]{1,0:T(8,128)(2,1)S(1)}, bf16[80,1024]{1,0:T(8,128)(2,1)S(1)}, u32[]{:S(2)}, u32[]{:S(2)}) %collective-permute-start.17) | collective-permute-done | bytes 163872 | tf_op jit(solution)/shard_map/ppermute | solution.py:890
  169.0 26.5 %shard_map.303 = (f32[640,2816]{1,0:T(8,128)}, f32[640,2816]{1,0:T(8,128)}, bf16[8,80,1024]{2,1,0:T(8,128)(2,1)}, bf16[640,1024]{1,0:T(8,128)(2,1)}, bf16[640,10...) custom-call(s32[1]{0:T(128)} %bitcast.refs_0_.own_ref, bf16[8,80,1152]{2,1,0:T(8,128)(2,1)} %all-to-all-done.1.refs_1_, ...), custom_call_target="tpu_custom_call" | custom-call | flops 24000000000 | bytes 35323904 | tf_op jit(solution)/shard_map/pallas_call | solution.py:732
  195.6 7.4 %all-to-all-start.3 = ((bf16[8,80,1024]{2,1,0:T(8,128)(2,1)}), bf16[8,80,1024]{2,1,0:T(8,128)(2,1)S(1)}, u32[]{:S(2)}, u32[]{:S(2)}) async-start(bf16[8,80,1024]{2,1,0:T(8,128)(2,1)} %get-tuple-element.165), calls=%async_computation.3 | async-start | bytes 2621440 | tf_op jit(solution)/shard_map/all_to_all | solution.py:988
  203.3 31.6 %shard_map.304 = (bf16[8,80,1024]{2,1,0:T(8,128)(2,1)}, bf16[1024,2816]{1,0:T(8,128)(2,1)}, bf16[2,256,2816]{2,1,0:T(8,128)(2,1)}, bf16[2,256,2816]{2,1,0:T(8,128)(2,1)}) custom-call(s32[1]{0:T(128)} %bitcast.refs_0_.own_ref, s32[1]{0:T(128)} %bitcast.1.refs_1_.refs_0_.me_ref, bf16[640,1024]{1,0:T(8,128)(2,1)} %get-tuple-element.166.slot_grad_ref, ...), custom_call_target="tpu_custom_call" | custom-call | flops 30000001024 | bytes 52625408 | tf_op jit(solution)/shard_map/pallas_call | solution.py:844
  235.9 6.0 %all-to-all-start.4 = ((bf16[8,80,1024]{2,1,0:T(8,128)(2,1)}), bf16[8,80,1024]{2,1,0:T(8,128)(2,1)S(1)}, u32[]{:S(2)}, u32[]{:S(2)}) async-start(bf16[8,80,1024]{2,1,0:T(8,128)(2,1)} %get-tuple-element.180), calls=%async_computation.4 | async-start | bytes 2621440 | tf_op jit(solution)/shard_map/all_to_all | solution.py:988
  246.6 22.9 %all-to-all-done.4 = bf16[8,80,1024]{2,1,0:T(8,128)(2,1)S(1)} async-done(((bf16[8,80,1024]{2,1,0:T(8,128)(2,1)}), bf16[8,80,1024]{2,1,0:T(8,128)(2,1)S(1)}, u32[]{:S(2)}, u32[]{:S(2)}) %all-to-all-start.4) | async-done | bytes 1310752 | tf_op jit(solution)/shard_map/all_to_all | solution.py:988
  270.6 7.2 %shard_map.306 = (f32[256,1024]{1,0:T(8,128)}, bf16[8,256,128]{2,1,0:T(8,128)(2,1)}, bf16[2,256,1152]{2,1,0:T(8,128)(2,1)}, bf16[2,256,1152]{2,1,0:T(8,128)(2,1)}) custom-call(s32[1]{0:T(128)} %bitcast.1.refs_1_.refs_0_.me_ref, f32[256,128]{1,0:T(8,128)} %get-tuple-element.179.refs_1_, bf16[1024,128]{1,0:T(8,128)(2,1)} %get-tuple-element.150.refs_3_.refs_2_.aux_ref, ...), custom_call_target="tpu_custom_call" | custom-call | flops 6000000000 | bytes 5505024 | tf_op jit(solution)/shard_map/pallas_call | solution.py:1145
  278.0 5.0 %all-to-all-start.5 = ((bf16[8,256,128]{2,1,0:T(8,128)(2,1)}), bf16[8,256,128]{2,1,0:T(8,128)(2,1)S(1)}, u32[]{:S(2)}, u32[]{:S(2)}) async-start(bf16[8,256,128]{2,1,0:T(8,128)(2,1)} %get-tuple-element.185), calls=%async_computation.6 | async-start | bytes 1048576 | tf_op jit(solution)/shard_map/all_to_all | solution.py:985
  283.0 5.0 %add_convert_fusion = bf16[2,256,2816]{2,1,0:T(8,128)(2,1)} fusion(bf16[2,256,2816]{2,1,0:T(8,128)(2,1)} %collective-permute-done.22, bf16[2,256,2816]{2,1,0:T(8,128)(2,1)} %get-tuple-element.188), kind=kLoop, calls=%fused_computation | loop fusion | flops 5767168 | bytes 8650752 | tf_op jit(solution)/shard_map/convert_element_type | solution.py:1118
  290.6 6.9 %all-to-all-done.5 = bf16[8,256,128]{2,1,0:T(8,128)(2,1)S(1)} async-done(((bf16[8,256,128]{2,1,0:T(8,128)(2,1)}), bf16[8,256,128]{2,1,0:T(8,128)(2,1)S(1)}, u32[]{:S(2)}, u32[]{:S(2)}) %all-to-all-start.5) | async-done | bytes 524320 | tf_op jit(solution)/shard_map/all_to_all | solution.py:985
  299.0 23.2 %shard_map.307 = (bf16[2048,384]{1,0:T(8,128)(2,1)}, bf16[2,272,384]{2,1,0:T(8,128)(2,1)}, bf16[2,272,384]{2,1,0:T(8,128)(2,1)}) custom-call(s32[1]{0:T(128)} %bitcast.1.refs_1_.refs_0_.me_ref, bf16[2048,128]{1,0:T(8,128)(2,1)} %bitcast.85, bf16[8,2,256,1280]{3,2,1,0:T(8,128)(2,1)} %get-tuple-element.191.refs_2_, ...), custom_call_target="tpu_custom_call" | custom-call | flops 60000002048 | bytes 13107200 | tf_op jit(solution)/shard_map/pallas_call | solution.py:398
  341.0 12.5 %collective-permute-done.26.refs_2_ = bf16[4,32,1536]{2,1,0:T(8,128)(2,1)S(1)} collective-permute-done((bf16[4,32,1536]{2,1,0:T(8,128)(2,1)S(1)}, bf16[4,32,1536]{2,1,0:T(8,128)(2,1)S(1)}, u32[]{:S(2)}, u32[]{:S(2)}) %collective-permute-start.26) | collective-permute-done | bytes 393248 | tf_op jit(solution)/shard_map/ppermute | solution.py:890
  354.4 4.9 %collective-permute-start.28 = (bf16[32,1920]{1,0:T(8,128)(2,1)S(1)}, bf16[32,1920]{1,0:T(8,128)(2,1)S(1)}, u32[]{:S(2)}, u32[]{:S(2)}) collective-permute-start(bf16[32,1920]{1,0:T(8,128)(2,1)S(1)} %get-tuple-element.207), channel_id=1, source_target_pairs={{0,4},{1,5},{2,6},{3,7},{4,0},{5,1},{6,2},{7,3},{8,12},{9,13},{10,... | collective-permute-start | bytes 368648 | tf_op jit(solution)/shard_map/ppermute | solution.py:890
  359.4 10.0 %all-to-all-done.6.blocks_ref = bf16[8,256,384]{2,1,0:T(8,128)(2,1)S(1)} async-done(((bf16[8,256,384]{2,1,0:T(8,128)(2,1)}), bf16[8,256,384]{2,1,0:T(8,128)(2,1)S(1)}, u32[]{:S(2)}, u32[]{:S(2)}) %all-to-all-start.6) | async-done | bytes 1572896 | tf_op jit(solution)/shard_map/all_to_all | solution.py:985
  373.5 4.8 %shard_map.310 = f32[256,1024]{1,0:T(8,128)} custom-call(bf16[8,256,384]{2,1,0:T(8,128)(2,1)S(1)} %all-to-all-done.6.blocks_ref, bf16[1024,3072]{1,0:T(8,128)(2,1)S(1)} %copy-done.23, bf16[256,1024]{1,0:T(8,128)(2,1)S(1)} %copy-done.11, bf16[1024,128]{1,0:T(8,128)(2,1)S(1)} %copy-done.34, f32[256,1024]{1,0:T(8,128)S(1)} %copy-done.30), custom_call_target="tpu_custom_call" | custom-call | flops 60000002048 | bytes 9437184 | tf_op jit(solution)/shard_map/pallas_call | solution.py:1174
  (259 shorter events, 104.5 us)
Async XLA Ops:
  7.2 161.1 %all-gather.10.cloned.1.call-start = ((), (), s32[]{:S(2)}) async-start(), calls=%async_computation.14 | async-start | bytes 7208960 | tf_op jit(solution)/shard_map/all_gather | solution.py:1005
  7.9 160.4 %all-gather.12.cloned.1.call-start = ((), (), s32[]{:S(2)}) async-start(), calls=%async_computation.15 | async-start | bytes 7208960 | tf_op jit(solution)/shard_map/all_gather | solution.py:1006
  8.8 159.6 %all-gather.14.cloned.1.call-start = ((), (), s32[]{:S(2)}) async-start(), calls=%async_computation.16 | async-start | bytes 7208960 | tf_op jit(solution)/shard_map/all_gather | solution.py:1007
  9.7 19.3 %collective-permute-start = (bf16[384,1024]{1,0:T(8,128)(2,1)S(1)}, bf16[384,1024]{1,0:T(8,128)(2,1)S(1)}, u32[]{:S(2)}, u32[]{:S(2)}) collective-permute-start(bf16[384,1024]{1,0:T(8,128)(2,1)S(1)} %constant_dynamic-update-slice_fusion.refs_1_.refs_2_), channel_id=1, source_target_pairs={{0,2},{2,4},{4,6},{6,7},{7,5},{5,3},{3,1},{1,0},{8,10},{10,12},{12... | collective-permute-start | bytes 2359304 | tf_op jit(solution)/shard_map/ppermute | solution.py:915
  9.8 19.3 %collective-permute-start.1 = (bf16[384,1024]{1,0:T(8,128)(2,1)S(1)}, bf16[384,1024]{1,0:T(8,128)(2,1)S(1)}, u32[]{:S(2)}, u32[]{:S(2)}) collective-permute-start(bf16[384,1024]{1,0:T(8,128)(2,1)S(1)} %constant_dynamic-update-slice_fusion.refs_1_.refs_2_), channel_id=1, source_target_pairs={{0,1},{2,0},{4,2},{6,4},{7,6},{5,7},{3,5},{1,3},{8,9},{10,8},{12,1... | collective-permute-start | bytes 2359304 | tf_op jit(solution)/shard_map/ppermute | solution.py:915
  29.1 27.0 %collective-permute-start.2 = (bf16[384,1024]{1,0:T(8,128)(2,1)S(1)}, bf16[384,1024]{1,0:T(8,128)(2,1)}, u32[]{:S(2)}, u32[]{:S(2)}) collective-permute-start(bf16[384,1024]{1,0:T(8,128)(2,1)S(1)} %collective-permute-done.refs_2_.refs_3_), channel_id=1, source_target_pairs={{0,2},{2,4},{4,6},{6,7},{7,5},{5,3},{3,1},{1,0},{8,10},{10,12},{12... | collective-permute-start | bytes 2359304 | tf_op jit(solution)/shard_map/ppermute | solution.py:915
  30.8 25.2 %collective-permute-start.3 = (bf16[384,1024]{1,0:T(8,128)(2,1)S(1)}, bf16[384,1024]{1,0:T(8,128)(2,1)S(1)}, u32[]{:S(2)}, u32[]{:S(2)}) collective-permute-start(bf16[384,1024]{1,0:T(8,128)(2,1)S(1)} %collective-permute-done.1.refs_7_.refs_8_), channel_id=1, source_target_pairs={{0,1},{2,0},{4,2},{6,4},{7,6},{5,7},{3,5},{1,3},{8,9},{10,8},{12,1... | collective-permute-start | bytes 2359304 | tf_op jit(solution)/shard_map/ppermute | solution.py:915
  31.9 24.2 %all-to-all-start = ((bf16[8,32,512]{2,1,0:T(8,128)(2,1)}), bf16[8,32,512]{2,1,0:T(8,128)(2,1)S(1)}, u32[]{:S(2)}, u32[]{:S(2)}) async-start(bf16[8,32,512]{2,1,0:T(8,128)(2,1)} %pad_maximum_fusion), calls=%async_computation | async-start | bytes 524288 | tf_op jit(solution)/shard_map/all_to_all | solution.py:988
  83.6 38.4 %all-to-all-start.1 = ((bf16[8,80,1152]{2,1,0:T(8,128)(2,1)}), bf16[8,80,1152]{2,1,0:T(8,128)(2,1)}, u32[]{:S(2)}, u32[]{:S(2)}) async-start(bf16[8,80,1152]{2,1,0:T(8,128)(2,1)} %shard_map.299), calls=%async_computation.1 | async-start | bytes 2949120 | tf_op jit(solution)/shard_map/all_to_all | solution.py:988
  88.7 106.9 %all-gather.8.cloned.1.call-start = ((), (), s32[]{:S(2)}) async-start(), calls=%async_computation.10 | async-start | bytes 7864320 | tf_op jit(solution)/shard_map/all_gather | solution.py:1101
  97.3 24.6 %collective-permute-start.11 = (bf16[256,1024]{1,0:T(8,128)(2,1)S(1)}, bf16[256,1024]{1,0:T(8,128)(2,1)S(1)}, u32[]{:S(2)}, u32[]{:S(2)}) collective-permute-start(bf16[256,1024]{1,0:T(8,128)(2,1)S(1)} %get-tuple-element.152.refs_5_.refs_7_), channel_id=1, source_target_pairs={{0,16},{8,24},{16,0},{24,8},{1,17},{9,25},{17,1},{25,9},{2,18},{10... | collective-permute-start | bytes 1572872 | tf_op jit(solution)/shard_map/ppermute | solution.py:890
  128.1 141.5 %reduce-scatter.4.cloned.1.call-start = ((), (), s32[]{:S(2)}) async-start(), calls=%async_computation.11 | async-start | bytes 7208960 | tf_op jit(solution)/shard_map/reduce_scatter | solution.py:1119
  146.4 21.8 %collective-permute-start.18 = (bf16[80,1024]{1,0:T(8,128)(2,1)S(1)}, bf16[80,1024]{1,0:T(8,128)(2,1)S(1)}, u32[]{:S(2)}, u32[]{:S(2)}) collective-permute-start(bf16[80,1024]{1,0:T(8,128)(2,1)S(1)} %get-tuple-element.159), channel_id=1, source_target_pairs={{0,5},{1,4},{2,7},{3,6},{4,1},{5,0},{6,3},{7,2},{8,13},{9,12},{10,... | collective-permute-start | bytes 491528 | tf_op jit(solution)/shard_map/ppermute | solution.py:890
  195.6 39.3 %all-to-all-start.3 = ((bf16[8,80,1024]{2,1,0:T(8,128)(2,1)}), bf16[8,80,1024]{2,1,0:T(8,128)(2,1)S(1)}, u32[]{:S(2)}, u32[]{:S(2)}) async-start(bf16[8,80,1024]{2,1,0:T(8,128)(2,1)} %get-tuple-element.165), calls=%async_computation.3 | async-start | bytes 2621440 | tf_op jit(solution)/shard_map/all_to_all | solution.py:988
  203.0 119.2 %reduce-scatter.6.cloned.1.call-start = ((), (), s32[]{:S(2)}) async-start(), calls=%async_computation.12 | async-start | bytes 7208960 | tf_op jit(solution)/shard_map/reduce_scatter | solution.py:1143
  235.9 33.6 %all-to-all-start.4 = ((bf16[8,80,1024]{2,1,0:T(8,128)(2,1)}), bf16[8,80,1024]{2,1,0:T(8,128)(2,1)S(1)}, u32[]{:S(2)}, u32[]{:S(2)}) async-start(bf16[8,80,1024]{2,1,0:T(8,128)(2,1)} %get-tuple-element.180), calls=%async_computation.4 | async-start | bytes 2621440 | tf_op jit(solution)/shard_map/all_to_all | solution.py:988
  241.9 41.1 %collective-permute-start.22 = (bf16[2,256,2816]{2,1,0:T(8,128)(2,1)}, bf16[2,256,2816]{2,1,0:T(8,128)(2,1)}, u32[]{:S(2)}, u32[]{:S(2)}) collective-permute-start(bf16[2,256,2816]{2,1,0:T(8,128)(2,1)} %get-tuple-element.189), channel_id=1, source_target_pairs={{0,8},{8,0},{16,24},{24,16},{1,9},{9,1},{17,25},{25,17},{2,10},{10... | collective-permute-start | bytes 8650760 | tf_op jit(solution)/shard_map/ppermute | solution.py:890
  278.0 19.5 %all-to-all-start.5 = ((bf16[8,256,128]{2,1,0:T(8,128)(2,1)}), bf16[8,256,128]{2,1,0:T(8,128)(2,1)S(1)}, u32[]{:S(2)}, u32[]{:S(2)}) async-start(bf16[8,256,128]{2,1,0:T(8,128)(2,1)} %get-tuple-element.185), calls=%async_computation.6 | async-start | bytes 1048576 | tf_op jit(solution)/shard_map/all_to_all | solution.py:985
  298.4 23.8 %collective-permute-start.23 = (bf16[1,256,1152]{2,1,0:T(8,128)(2,1)S(1)}, bf16[1,256,1152]{2,1,0:T(8,128)(2,1)S(1)}, u32[]{:S(2)}, u32[]{:S(2)}) collective-permute-start(bf16[1,256,1152]{2,1,0:T(8,128)(2,1)S(1)} %get-tuple-element.230), channel_id=1, source_target_pairs={{0,16},{8,24},{16,0},{24,8},{1,17},{9,25},{17,1},{25,9},{2,18},{10... | collective-permute-start | bytes 1769480 | tf_op jit(solution)/shard_map/ppermute | solution.py:890
  322.2 47.1 %all-to-all-start.6 = ((bf16[8,256,384]{2,1,0:T(8,128)(2,1)}), bf16[8,256,384]{2,1,0:T(8,128)(2,1)S(1)}, u32[]{:S(2)}, u32[]{:S(2)}) async-start(bf16[8,256,384]{2,1,0:T(8,128)(2,1)} %bitcast.82), calls=%async_computation.8 | async-start | bytes 3145728 | tf_op jit(solution)/shard_map/all_to_all | solution.py:985
  326.7 51.7 %reduce-scatter.8.cloned.1.call-start = ((), (), s32[]{:S(2)}) async-start(), calls=%async_computation.13 | async-start | bytes 4325376 | tf_op jit(solution)/shard_map/reduce_scatter | solution.py:1139
  353.6 28.0 %collective-permute-start.27 = (bf16[32,1920]{1,0:T(8,128)(2,1)S(1)}, bf16[32,1920]{1,0:T(8,128)(2,1)S(1)}, u32[]{:S(2)}, u32[]{:S(2)}) collective-permute-start(bf16[32,1920]{1,0:T(8,128)(2,1)S(1)} %get-tuple-element.206), channel_id=1, source_target_pairs={{0,2},{1,3},{2,0},{3,1},{4,6},{5,7},{6,4},{7,5},{8,10},{9,11},{10,... | collective-permute-start | bytes 368648 | tf_op jit(solution)/shard_map/ppermute | solution.py:890
  354.4 27.1 %collective-permute-start.28 = (bf16[32,1920]{1,0:T(8,128)(2,1)S(1)}, bf16[32,1920]{1,0:T(8,128)(2,1)S(1)}, u32[]{:S(2)}, u32[]{:S(2)}) collective-permute-start(bf16[32,1920]{1,0:T(8,128)(2,1)S(1)} %get-tuple-element.207), channel_id=1, source_target_pairs={{0,4},{1,5},{2,6},{3,7},{4,0},{5,1},{6,2},{7,3},{8,12},{9,13},{10,... | collective-permute-start | bytes 368648 | tf_op jit(solution)/shard_map/ppermute | solution.py:890
  359.4 22.2 %collective-permute-start.29 = (bf16[32,1920]{1,0:T(8,128)(2,1)S(1)}, bf16[32,1920]{1,0:T(8,128)(2,1)S(1)}, u32[]{:S(2)}, u32[]{:S(2)}) collective-permute-start(bf16[32,1920]{1,0:T(8,128)(2,1)S(1)} %get-tuple-element.208), channel_id=1, source_target_pairs={{0,6},{1,7},{2,4},{3,5},{4,2},{5,3},{6,0},{7,1},{8,14},{9,15},{10,... | collective-permute-start | bytes 368648 | tf_op jit(solution)/shard_map/ppermute | solution.py:890
  (83 other events, 872.5 us)
Sparse Core Ops, SparseCore 0:
  9.6 44.5 all-gather.9
  55.8 44.6 all-gather.11
  102.0 43.5 all-gather.13
  147.6 46.3 all-gather.7
  196.4 55.5 reduce-scatter.3
  254.5 62.0 reduce-scatter.5
  330.3 41.0 reduce-scatter.7
where the time goes:
time: 396 us; the launch traced here: 390 us
  Pallas kernels  132 us (33%)
  waiting for transfers between devices  123 us (31%)
  starting transfers between devices  74.8 us (19%)
  local copies, waits for them, and re-layouts  23 us (6%)
  other arithmetic  19.4 us (5%)
  between operations  15.2 us (4%)
    all_to_all x4, waiting for transfers between devices, exchange_all(): return lax.all_to_all(blocks, 'expert', 0, 0, tiled=True)  36.5 us
    ppermute x22, waiting for transfers between devices, flip(): return lax.ppermute(values, axis, [(k, k ^ mask) for k in range(n)])  32.6 us
    pallas_call x1, Pallas kernels, expert_backward(): call(expert_back_kernel, [struct((groups, count // groups, width), BF), s...  31.6 us
    ppermute x8, waiting for transfers between devices, move(): return lax.ppermute(values, 'expert', pairs)  27.8 us
    pallas_call x1, Pallas kernels, expert_forward(): call(lambda *refs: expert_kernel(groups, *refs), (struct((count, ff), F32...  26.5 us
    ppermute x22, starting transfers between devices, flip(): return lax.ppermute(values, axis, [(k, k ^ mask) for k in range(n)])  25.3 us
    all_to_all x4, starting transfers between devices, exchange_all(): return lax.all_to_all(blocks, 'expert', 0, 0, tiled=True)  25.1 us
    all_to_all x3, waiting for transfers between devices, exchange(): lax.all_to_all(blocks, 'expert', 0, 0, axis_index_groups=teams, tiled=True)  23.6 us
  transfers between devices with their start and end apart: 44, of which 20 were waited for; matrix products, arithmetic and copies ran while one was open for 7% of the time, Pallas kernels for 33%

commit v1 on v0

--- a/solution.py
+++ b/solution.py
@@ -1177,7 +1177,7 @@
         60e9,
         6 * width * width + 12 * length * width,
         grid=(3,),
-        mib=24, in_specs=[
+        in_specs=[
             pl.BlockSpec(grads_here.shape, lambda part: (0, 0, 0)),
             pl.BlockSpec((width, width), lambda part: (0, part)),
             pl.BlockSpec((length, width), fixed),

time: 396 us -> 396 us (level)
  local copies, waits for them, and re-layouts: 23 us -> 18.1 us
    unnamed x132 -> x130, local copies, waits for them, and re-layouts: 18.4 us -> 13.4 us
  transfers between devices with their start and end apart: 44 -> 44, of which waited for: 20 -> 20; matrix products, arithmetic and copies ran while one was open for 7% -> 7% of each run, Pallas kernels for 33% -> 34%
where the time goes in v1:
time: 396 us; the launch traced here: 390 us
  Pallas kernels  134 us (34%)
  waiting for transfers between devices  126 us (32%)
  starting transfers between devices  74.9 us (19%)
  other arithmetic  18.6 us (5%)
  local copies, waits for them, and re-layouts  18.1 us (5%)
  between operations  15.2 us (4%)
    all_to_all x4, waiting for transfers between devices, exchange_all(): return lax.all_to_all(blocks, 'expert', 0, 0, tiled=True)  36.4 us
    ppermute x22, waiting for transfers between devices, flip(): return lax.ppermute(values, axis, [(k, k ^ mask) for k in range(n)])  33.5 us
    pallas_call x1, Pallas kernels, expert_backward(): call(expert_back_kernel, [struct((groups, count // groups, width), BF), s...  31.6 us
    ppermute x8, waiting for transfers between devices, move(): return lax.ppermute(values, 'expert', pairs)  27.8 us
    pallas_call x1, Pallas kernels, expert_forward(): call(lambda *refs: expert_kernel(groups, *refs), (struct((count, ff), F32...  26.6 us
    all_to_all x3, waiting for transfers between devices, exchange(): lax.all_to_all(blocks, 'expert', 0, 0, axis_index_groups=teams, tiled=True)  25.3 us
    all_to_all x4, starting transfers between devices, exchange_all(): return lax.all_to_all(blocks, 'expert', 0, 0, tiled=True)  25.1 us
    ppermute x22, starting transfers between devices, flip(): return lax.ppermute(values, axis, [(k, k ^ mask) for k in range(n)])  24.8 us
  transfers between devices with their start and end apart: 44, of which 20 were waited for; matrix products, arithmetic and copies ran while one was open for 7% of the time, Pallas kernels for 34%

profile of v1, /device:TPU:4, one launch (start us, length us, event | category | flops | bytes accessed | tf_op | source)
XLA Modules:
  0.0 389.6 jit_solution(13201383995066157929)
XLA Ops:
  12.0 17.1 %collective-permute-done.refs_2_.refs_3_ = bf16[384,1024]{1,0:T(8,128)(2,1)S(1)} collective-permute-done((bf16[384,1024]{1,0:T(8,128)(2,1)S(1)}, bf16[384,1024]{1,0:T(8,128)(2,1)S(1)}, u32[]{:S(2)}, u32[]{:S(2)}) %collective-permute-start) | collective-permute-done | bytes 786464 | tf_op jit(solution)/shard_map/ppermute | solution.py:915
  31.9 6.6 %all-to-all-start = ((bf16[8,32,512]{2,1,0:T(8,128)(2,1)}), bf16[8,32,512]{2,1,0:T(8,128)(2,1)S(1)}, u32[]{:S(2)}, u32[]{:S(2)}) async-start(bf16[8,32,512]{2,1,0:T(8,128)(2,1)} %pad_maximum_fusion), calls=%async_computation | async-start | bytes 524288 | tf_op jit(solution)/shard_map/all_to_all | solution.py:988
  42.5 13.6 %all-to-all-done = bf16[8,32,512]{2,1,0:T(8,128)(2,1)S(1)} async-done(((bf16[8,32,512]{2,1,0:T(8,128)(2,1)}), bf16[8,32,512]{2,1,0:T(8,128)(2,1)S(1)}, u32[]{:S(2)}, u32[]{:S(2)}) %all-to-all-start) | async-done | bytes 262176 | tf_op jit(solution)/shard_map/all_to_all | solution.py:988
  76.0 5.7 %collective-permute-done.10.refs_9_.refs_10_ = bf16[192,1024]{1,0:T(8,128)(2,1)S(1)} collective-permute-done((bf16[192,1024]{1,0:T(8,128)(2,1)S(1)}, bf16[192,1024]{1,0:T(8,128)(2,1)S(1)}, u32[]{:S(2)}, u32[]{:S(2)}) %collective-permute-start.10) | collective-permute-done | bytes 393248 | tf_op jit(solution)/shard_map/ppermute | solution.py:915
  83.6 5.1 %all-to-all-start.1 = ((bf16[8,80,1152]{2,1,0:T(8,128)(2,1)}), bf16[8,80,1152]{2,1,0:T(8,128)(2,1)}, u32[]{:S(2)}, u32[]{:S(2)}) async-start(bf16[8,80,1152]{2,1,0:T(8,128)(2,1)} %shard_map.299), calls=%async_computation.1 | async-start | bytes 2949120 | tf_op jit(solution)/shard_map/all_to_all | solution.py:988
  98.8 23.1 %shard_map.301 = (bf16[2048,1024]{1,0:T(8,128)(2,1)}, bf16[2048,384]{1,0:T(8,128)(2,1)}, bf16[8,2,256,1280]{3,2,1,0:T(8,128)(2,1)}, bf16[2048,128]{1,0:T(8,128)(...) custom-call(s32[8]{0:T(128)} %copy-done.22, s32[1]{0:T(128)} %bitcast.1.refs_1_.refs_0_.me_ref, ...), custom_call_target="tpu_custom_call" | custom-call | flops 24000000000 | bytes 27262976 | tf_op jit(solution)/shard_map/pallas_call | solution.py:230
  122.0 6.1 %all-to-all-start.2 = ((bf16[8,256,128]{2,1,0:T(8,128)(2,1)}), bf16[8,256,128]{2,1,0:T(8,128)(2,1)S(1)}, u32[]{:S(2)}, u32[]{:S(2)}) async-start(bf16[8,256,128]{2,1,0:T(8,128)(2,1)} %bitcast.18), calls=%async_computation.2 | async-start | bytes 1048576 | tf_op jit(solution)/shard_map/all_to_all | solution.py:985
  131.1 6.7 %all-to-all-done.2.refs_1_ = bf16[8,256,128]{2,1,0:T(8,128)(2,1)S(1)} async-done(((bf16[8,256,128]{2,1,0:T(8,128)(2,1)}), bf16[8,256,128]{2,1,0:T(8,128)(2,1)S(1)}, u32[]{:S(2)}, u32[]{:S(2)}) %all-to-all-start.2) | async-done | bytes 524320 | tf_op jit(solution)/shard_map/all_to_all | solution.py:985
  152.0 6.2 %collective-permute-start.20 = (bf16[80,1024]{1,0:T(8,128)(2,1)S(1)}, bf16[80,1024]{1,0:T(8,128)(2,1)S(1)}, u32[]{:S(2)}, u32[]{:S(2)}) collective-permute-start(bf16[80,1024]{1,0:T(8,128)(2,1)S(1)} %get-tuple-element.161), channel_id=1, source_target_pairs={{0,7},{1,6},{2,5},{3,4},{4,3},{5,2},{6,1},{7,0},{8,15},{9,14},{10,... | collective-permute-start | bytes 491528 | tf_op jit(solution)/shard_map/ppermute | solution.py:890
  158.2 6.1 %collective-permute-done.17.refs_10_ = bf16[80,1024]{1,0:T(8,128)(2,1)S(1)} collective-permute-done((bf16[80,1024]{1,0:T(8,128)(2,1)S(1)}, bf16[80,1024]{1,0:T(8,128)(2,1)S(1)}, u32[]{:S(2)}, u32[]{:S(2)}) %collective-permute-start.17) | collective-permute-done | bytes 163872 | tf_op jit(solution)/shard_map/ppermute | solution.py:890
  169.0 26.6 %shard_map.303 = (f32[640,2816]{1,0:T(8,128)}, f32[640,2816]{1,0:T(8,128)}, bf16[8,80,1024]{2,1,0:T(8,128)(2,1)}, bf16[640,1024]{1,0:T(8,128)(2,1)}, bf16[640,10...) custom-call(s32[1]{0:T(128)} %bitcast.refs_0_.own_ref, bf16[8,80,1152]{2,1,0:T(8,128)(2,1)} %all-to-all-done.1.refs_1_, ...), custom_call_target="tpu_custom_call" | custom-call | flops 24000000000 | bytes 35323904 | tf_op jit(solution)/shard_map/pallas_call | solution.py:732
  195.7 7.4 %all-to-all-start.3 = ((bf16[8,80,1024]{2,1,0:T(8,128)(2,1)}), bf16[8,80,1024]{2,1,0:T(8,128)(2,1)S(1)}, u32[]{:S(2)}, u32[]{:S(2)}) async-start(bf16[8,80,1024]{2,1,0:T(8,128)(2,1)} %get-tuple-element.165), calls=%async_computation.3 | async-start | bytes 2621440 | tf_op jit(solution)/shard_map/all_to_all | solution.py:988
  203.3 31.6 %shard_map.304 = (bf16[8,80,1024]{2,1,0:T(8,128)(2,1)}, bf16[1024,2816]{1,0:T(8,128)(2,1)}, bf16[2,256,2816]{2,1,0:T(8,128)(2,1)}, bf16[2,256,2816]{2,1,0:T(8,128)(2,1)}) custom-call(s32[1]{0:T(128)} %bitcast.refs_0_.own_ref, s32[1]{0:T(128)} %bitcast.1.refs_1_.refs_0_.me_ref, bf16[640,1024]{1,0:T(8,128)(2,1)} %get-tuple-element.166.slot_grad_ref, ...), custom_call_target="tpu_custom_call" | custom-call | flops 30000001024 | bytes 52625408 | tf_op jit(solution)/shard_map/pallas_call | solution.py:844
  236.0 6.0 %all-to-all-start.4 = ((bf16[8,80,1024]{2,1,0:T(8,128)(2,1)}), bf16[8,80,1024]{2,1,0:T(8,128)(2,1)S(1)}, u32[]{:S(2)}, u32[]{:S(2)}) async-start(bf16[8,80,1024]{2,1,0:T(8,128)(2,1)} %get-tuple-element.180), calls=%async_computation.4 | async-start | bytes 2621440 | tf_op jit(solution)/shard_map/all_to_all | solution.py:988
  246.7 22.9 %all-to-all-done.4 = bf16[8,80,1024]{2,1,0:T(8,128)(2,1)S(1)} async-done(((bf16[8,80,1024]{2,1,0:T(8,128)(2,1)}), bf16[8,80,1024]{2,1,0:T(8,128)(2,1)S(1)}, u32[]{:S(2)}, u32[]{:S(2)}) %all-to-all-start.4) | async-done | bytes 1310752 | tf_op jit(solution)/shard_map/all_to_all | solution.py:988
  270.6 7.4 %shard_map.306 = (f32[256,1024]{1,0:T(8,128)}, bf16[8,256,128]{2,1,0:T(8,128)(2,1)}, bf16[2,256,1152]{2,1,0:T(8,128)(2,1)}, bf16[2,256,1152]{2,1,0:T(8,128)(2,1)}) custom-call(s32[1]{0:T(128)} %bitcast.1.refs_1_.refs_0_.me_ref, f32[256,128]{1,0:T(8,128)} %get-tuple-element.179.refs_1_, bf16[1024,128]{1,0:T(8,128)(2,1)} %get-tuple-element.150.refs_3_.refs_2_.aux_ref, ...), custom_call_target="tpu_custom_call" | custom-call | flops 6000000000 | bytes 5505024 | tf_op jit(solution)/shard_map/pallas_call | solution.py:1145
  278.1 5.0 %all-to-all-start.5 = ((bf16[8,256,128]{2,1,0:T(8,128)(2,1)}), bf16[8,256,128]{2,1,0:T(8,128)(2,1)S(1)}, u32[]{:S(2)}, u32[]{:S(2)}) async-start(bf16[8,256,128]{2,1,0:T(8,128)(2,1)} %get-tuple-element.185), calls=%async_computation.6 | async-start | bytes 1048576 | tf_op jit(solution)/shard_map/all_to_all | solution.py:985
  289.1 8.6 %all-to-all-done.5 = bf16[8,256,128]{2,1,0:T(8,128)(2,1)S(1)} async-done(((bf16[8,256,128]{2,1,0:T(8,128)(2,1)}), bf16[8,256,128]{2,1,0:T(8,128)(2,1)S(1)}, u32[]{:S(2)}, u32[]{:S(2)}) %all-to-all-start.5) | async-done | bytes 524320 | tf_op jit(solution)/shard_map/all_to_all | solution.py:985
  298.5 23.1 %shard_map.307 = (bf16[2048,384]{1,0:T(8,128)(2,1)}, bf16[2,272,384]{2,1,0:T(8,128)(2,1)}, bf16[2,272,384]{2,1,0:T(8,128)(2,1)}) custom-call(s32[1]{0:T(128)} %bitcast.1.refs_1_.refs_0_.me_ref, bf16[2048,128]{1,0:T(8,128)(2,1)} %bitcast.85, bf16[8,2,256,1280]{3,2,1,0:T(8,128)(2,1)} %get-tuple-element.191.refs_2_, ...), custom_call_target="tpu_custom_call" | custom-call | flops 60000002048 | bytes 13107200 | tf_op jit(solution)/shard_map/pallas_call | solution.py:398
  321.6 5.1 %all-to-all-start.6 = ((bf16[8,256,384]{2,1,0:T(8,128)(2,1)}), bf16[8,256,384]{2,1,0:T(8,128)(2,1)S(1)}, u32[]{:S(2)}, u32[]{:S(2)}) async-start(bf16[8,256,384]{2,1,0:T(8,128)(2,1)} %bitcast.82), calls=%async_computation.8 | async-start | bytes 3145728 | tf_op jit(solution)/shard_map/all_to_all | solution.py:985
  340.8 12.7 %collective-permute-done.26.refs_2_ = bf16[4,32,1536]{2,1,0:T(8,128)(2,1)S(1)} collective-permute-done((bf16[4,32,1536]{2,1,0:T(8,128)(2,1)S(1)}, bf16[4,32,1536]{2,1,0:T(8,128)(2,1)S(1)}, u32[]{:S(2)}, u32[]{:S(2)}) %collective-permute-start.26) | collective-permute-done | bytes 393248 | tf_op jit(solution)/shard_map/ppermute | solution.py:890
  354.5 4.9 %collective-permute-start.28 = (bf16[32,1920]{1,0:T(8,128)(2,1)S(1)}, bf16[32,1920]{1,0:T(8,128)(2,1)S(1)}, u32[]{:S(2)}, u32[]{:S(2)}) collective-permute-start(bf16[32,1920]{1,0:T(8,128)(2,1)S(1)} %get-tuple-element.207), channel_id=1, source_target_pairs={{0,4},{1,5},{2,6},{3,7},{4,0},{5,1},{6,2},{7,3},{8,12},{9,13},{10,... | collective-permute-start | bytes 368648 | tf_op jit(solution)/shard_map/ppermute | solution.py:890
  359.4 10.0 %all-to-all-done.6.blocks_ref = bf16[8,256,384]{2,1,0:T(8,128)(2,1)S(1)} async-done(((bf16[8,256,384]{2,1,0:T(8,128)(2,1)}), bf16[8,256,384]{2,1,0:T(8,128)(2,1)S(1)}, u32[]{:S(2)}, u32[]{:S(2)}) %all-to-all-start.6) | async-done | bytes 1572896 | tf_op jit(solution)/shard_map/all_to_all | solution.py:985
  370.6 7.5 %shard_map.310 = f32[256,1024]{1,0:T(8,128)} custom-call(bf16[8,256,384]{2,1,0:T(8,128)(2,1)} %copy-done.34, bf16[1024,3072]{1,0:T(8,128)(2,1)} %all-gather.8.cloned.1.call-done.w_ref, bf16[256,1024]{1,0:T(8,128)(2,1)} %tok_ref.1, bf16[1024,128]{1,0:T(8,128)(2,1)} %get-tuple-element.150.refs_3_.refs_2_.aux_ref, f32[256,1024]{1,0:T(8,128)} %get-tuple-element.211.resid_grad_ref), custom_call_target="tpu_custom_call" | custom-call | flops 60000002048 | bytes 9437184 | tf_op jit(solution)/shard_map/pallas_call | solution.py:1174
  (257 shorter events, 99.4 us)
Async XLA Ops:
  7.2 161.1 %all-gather.10.cloned.1.call-start = ((), (), s32[]{:S(2)}) async-start(), calls=%async_computation.14 | async-start | bytes 7208960 | tf_op jit(solution)/shard_map/all_gather | solution.py:1005
  7.9 160.4 %all-gather.12.cloned.1.call-start = ((), (), s32[]{:S(2)}) async-start(), calls=%async_computation.15 | async-start | bytes 7208960 | tf_op jit(solution)/shard_map/all_gather | solution.py:1006
  8.8 159.6 %all-gather.14.cloned.1.call-start = ((), (), s32[]{:S(2)}) async-start(), calls=%async_computation.16 | async-start | bytes 7208960 | tf_op jit(solution)/shard_map/all_gather | solution.py:1007
  9.7 19.3 %collective-permute-start = (bf16[384,1024]{1,0:T(8,128)(2,1)S(1)}, bf16[384,1024]{1,0:T(8,128)(2,1)S(1)}, u32[]{:S(2)}, u32[]{:S(2)}) collective-permute-start(bf16[384,1024]{1,0:T(8,128)(2,1)S(1)} %constant_dynamic-update-slice_fusion.refs_1_.refs_2_), channel_id=1, source_target_pairs={{0,2},{2,4},{4,6},{6,7},{7,5},{5,3},{3,1},{1,0},{8,10},{10,12},{12... | collective-permute-start | bytes 2359304 | tf_op jit(solution)/shard_map/ppermute | solution.py:915
  9.8 19.3 %collective-permute-start.1 = (bf16[384,1024]{1,0:T(8,128)(2,1)S(1)}, bf16[384,1024]{1,0:T(8,128)(2,1)S(1)}, u32[]{:S(2)}, u32[]{:S(2)}) collective-permute-start(bf16[384,1024]{1,0:T(8,128)(2,1)S(1)} %constant_dynamic-update-slice_fusion.refs_1_.refs_2_), channel_id=1, source_target_pairs={{0,1},{2,0},{4,2},{6,4},{7,6},{5,7},{3,5},{1,3},{8,9},{10,8},{12,1... | collective-permute-start | bytes 2359304 | tf_op jit(solution)/shard_map/ppermute | solution.py:915
  29.1 27.0 %collective-permute-start.2 = (bf16[384,1024]{1,0:T(8,128)(2,1)S(1)}, bf16[384,1024]{1,0:T(8,128)(2,1)}, u32[]{:S(2)}, u32[]{:S(2)}) collective-permute-start(bf16[384,1024]{1,0:T(8,128)(2,1)S(1)} %collective-permute-done.refs_2_.refs_3_), channel_id=1, source_target_pairs={{0,2},{2,4},{4,6},{6,7},{7,5},{5,3},{3,1},{1,0},{8,10},{10,12},{12... | collective-permute-start | bytes 2359304 | tf_op jit(solution)/shard_map/ppermute | solution.py:915
  30.8 25.2 %collective-permute-start.3 = (bf16[384,1024]{1,0:T(8,128)(2,1)S(1)}, bf16[384,1024]{1,0:T(8,128)(2,1)S(1)}, u32[]{:S(2)}, u32[]{:S(2)}) collective-permute-start(bf16[384,1024]{1,0:T(8,128)(2,1)S(1)} %collective-permute-done.1.refs_7_.refs_8_), channel_id=1, source_target_pairs={{0,1},{2,0},{4,2},{6,4},{7,6},{5,7},{3,5},{1,3},{8,9},{10,8},{12,1... | collective-permute-start | bytes 2359304 | tf_op jit(solution)/shard_map/ppermute | solution.py:915
  31.9 24.2 %all-to-all-start = ((bf16[8,32,512]{2,1,0:T(8,128)(2,1)}), bf16[8,32,512]{2,1,0:T(8,128)(2,1)S(1)}, u32[]{:S(2)}, u32[]{:S(2)}) async-start(bf16[8,32,512]{2,1,0:T(8,128)(2,1)} %pad_maximum_fusion), calls=%async_computation | async-start | bytes 524288 | tf_op jit(solution)/shard_map/all_to_all | solution.py:988
  83.6 38.4 %all-to-all-start.1 = ((bf16[8,80,1152]{2,1,0:T(8,128)(2,1)}), bf16[8,80,1152]{2,1,0:T(8,128)(2,1)}, u32[]{:S(2)}, u32[]{:S(2)}) async-start(bf16[8,80,1152]{2,1,0:T(8,128)(2,1)} %shard_map.299), calls=%async_computation.1 | async-start | bytes 2949120 | tf_op jit(solution)/shard_map/all_to_all | solution.py:988
  88.7 107.0 %all-gather.8.cloned.1.call-start = ((), (), s32[]{:S(2)}) async-start(), calls=%async_computation.10 | async-start | bytes 7864320 | tf_op jit(solution)/shard_map/all_gather | solution.py:1101
  97.3 24.6 %collective-permute-start.11 = (bf16[256,1024]{1,0:T(8,128)(2,1)S(1)}, bf16[256,1024]{1,0:T(8,128)(2,1)S(1)}, u32[]{:S(2)}, u32[]{:S(2)}) collective-permute-start(bf16[256,1024]{1,0:T(8,128)(2,1)S(1)} %get-tuple-element.152.refs_5_.refs_7_), channel_id=1, source_target_pairs={{0,16},{8,24},{16,0},{24,8},{1,17},{9,25},{17,1},{25,9},{2,18},{10... | collective-permute-start | bytes 1572872 | tf_op jit(solution)/shard_map/ppermute | solution.py:890
  128.1 141.5 %reduce-scatter.4.cloned.1.call-start = ((), (), s32[]{:S(2)}) async-start(), calls=%async_computation.11 | async-start | bytes 7208960 | tf_op jit(solution)/shard_map/reduce_scatter | solution.py:1119
  146.4 21.8 %collective-permute-start.18 = (bf16[80,1024]{1,0:T(8,128)(2,1)S(1)}, bf16[80,1024]{1,0:T(8,128)(2,1)S(1)}, u32[]{:S(2)}, u32[]{:S(2)}) collective-permute-start(bf16[80,1024]{1,0:T(8,128)(2,1)S(1)} %get-tuple-element.159), channel_id=1, source_target_pairs={{0,5},{1,4},{2,7},{3,6},{4,1},{5,0},{6,3},{7,2},{8,13},{9,12},{10,... | collective-permute-start | bytes 491528 | tf_op jit(solution)/shard_map/ppermute | solution.py:890
  195.7 39.3 %all-to-all-start.3 = ((bf16[8,80,1024]{2,1,0:T(8,128)(2,1)}), bf16[8,80,1024]{2,1,0:T(8,128)(2,1)S(1)}, u32[]{:S(2)}, u32[]{:S(2)}) async-start(bf16[8,80,1024]{2,1,0:T(8,128)(2,1)} %get-tuple-element.165), calls=%async_computation.3 | async-start | bytes 2621440 | tf_op jit(solution)/shard_map/all_to_all | solution.py:988
  203.1 118.5 %reduce-scatter.6.cloned.1.call-start = ((), (), s32[]{:S(2)}) async-start(), calls=%async_computation.12 | async-start | bytes 7208960 | tf_op jit(solution)/shard_map/reduce_scatter | solution.py:1143
  236.0 33.5 %all-to-all-start.4 = ((bf16[8,80,1024]{2,1,0:T(8,128)(2,1)}), bf16[8,80,1024]{2,1,0:T(8,128)(2,1)S(1)}, u32[]{:S(2)}, u32[]{:S(2)}) async-start(bf16[8,80,1024]{2,1,0:T(8,128)(2,1)} %get-tuple-element.180), calls=%async_computation.4 | async-start | bytes 2621440 | tf_op jit(solution)/shard_map/all_to_all | solution.py:988
  242.0 41.2 %collective-permute-start.22 = (bf16[2,256,2816]{2,1,0:T(8,128)(2,1)}, bf16[2,256,2816]{2,1,0:T(8,128)(2,1)}, u32[]{:S(2)}, u32[]{:S(2)}) collective-permute-start(bf16[2,256,2816]{2,1,0:T(8,128)(2,1)} %get-tuple-element.189), channel_id=1, source_target_pairs={{0,8},{8,0},{16,24},{24,16},{1,9},{9,1},{17,25},{25,17},{2,10},{10... | collective-permute-start | bytes 8650760 | tf_op jit(solution)/shard_map/ppermute | solution.py:890
  278.1 19.6 %all-to-all-start.5 = ((bf16[8,256,128]{2,1,0:T(8,128)(2,1)}), bf16[8,256,128]{2,1,0:T(8,128)(2,1)S(1)}, u32[]{:S(2)}, u32[]{:S(2)}) async-start(bf16[8,256,128]{2,1,0:T(8,128)(2,1)} %get-tuple-element.185), calls=%async_computation.6 | async-start | bytes 1048576 | tf_op jit(solution)/shard_map/all_to_all | solution.py:985
  297.8 23.8 %collective-permute-start.23 = (bf16[1,256,1152]{2,1,0:T(8,128)(2,1)S(1)}, bf16[1,256,1152]{2,1,0:T(8,128)(2,1)S(1)}, u32[]{:S(2)}, u32[]{:S(2)}) collective-permute-start(bf16[1,256,1152]{2,1,0:T(8,128)(2,1)S(1)} %get-tuple-element.230), channel_id=1, source_target_pairs={{0,16},{8,24},{16,0},{24,8},{1,17},{9,25},{17,1},{25,9},{2,18},{10... | collective-permute-start | bytes 1769480 | tf_op jit(solution)/shard_map/ppermute | solution.py:890
  321.6 47.8 %all-to-all-start.6 = ((bf16[8,256,384]{2,1,0:T(8,128)(2,1)}), bf16[8,256,384]{2,1,0:T(8,128)(2,1)S(1)}, u32[]{:S(2)}, u32[]{:S(2)}) async-start(bf16[8,256,384]{2,1,0:T(8,128)(2,1)} %bitcast.82), calls=%async_computation.8 | async-start | bytes 3145728 | tf_op jit(solution)/shard_map/all_to_all | solution.py:985
  326.7 51.4 %reduce-scatter.8.cloned.1.call-start = ((), (), s32[]{:S(2)}) async-start(), calls=%async_computation.13 | async-start | bytes 4325376 | tf_op jit(solution)/shard_map/reduce_scatter | solution.py:1139
  353.6 27.7 %collective-permute-start.27 = (bf16[32,1920]{1,0:T(8,128)(2,1)S(1)}, bf16[32,1920]{1,0:T(8,128)(2,1)S(1)}, u32[]{:S(2)}, u32[]{:S(2)}) collective-permute-start(bf16[32,1920]{1,0:T(8,128)(2,1)S(1)} %get-tuple-element.206), channel_id=1, source_target_pairs={{0,2},{1,3},{2,0},{3,1},{4,6},{5,7},{6,4},{7,5},{8,10},{9,11},{10,... | collective-permute-start | bytes 368648 | tf_op jit(solution)/shard_map/ppermute | solution.py:890
  354.5 26.8 %collective-permute-start.28 = (bf16[32,1920]{1,0:T(8,128)(2,1)S(1)}, bf16[32,1920]{1,0:T(8,128)(2,1)S(1)}, u32[]{:S(2)}, u32[]{:S(2)}) collective-permute-start(bf16[32,1920]{1,0:T(8,128)(2,1)S(1)} %get-tuple-element.207), channel_id=1, source_target_pairs={{0,4},{1,5},{2,6},{3,7},{4,0},{5,1},{6,2},{7,3},{8,12},{9,13},{10,... | collective-permute-start | bytes 368648 | tf_op jit(solution)/shard_map/ppermute | solution.py:890
  359.4 21.9 %collective-permute-start.29 = (bf16[32,1920]{1,0:T(8,128)(2,1)S(1)}, bf16[32,1920]{1,0:T(8,128)(2,1)S(1)}, u32[]{:S(2)}, u32[]{:S(2)}) collective-permute-start(bf16[32,1920]{1,0:T(8,128)(2,1)S(1)} %get-tuple-element.208), channel_id=1, source_target_pairs={{0,6},{1,7},{2,4},{3,5},{4,2},{5,3},{6,0},{7,1},{8,14},{9,15},{10,... | collective-permute-start | bytes 368648 | tf_op jit(solution)/shard_map/ppermute | solution.py:890
  (82 other events, 865.1 us)
Sparse Core Ops, SparseCore 0:
  9.6 44.5 all-gather.9
  55.8 44.6 all-gather.11
  102.0 43.5 all-gather.13
  147.6 46.3 all-gather.7
  196.4 55.6 reduce-scatter.3
  254.6 62.6 reduce-scatter.5
  330.4 40.3 reduce-scatter.7
